TPU v7x, 32 devices: a whole 2x2x4 slice. The times are simulated.
32 devices in a mesh: row: 4 (over y, core), col: 8 (over z, x).
Axes of the slice: x: 2, y: 2, z: 4, core: 2. Of those that a mesh axis runs over, the one named last changes fastest.
Arguments:
- x_slots: bfloat16 [4, 16, 128, 128, 128], P('row', 'col'), may hold values from -0.875 to 0.875
- block_pairs: int32 [4, 16], replicated, may hold values from -1 to 15, as said below
- greens: bfloat16 [2, 512, 512], replicated, may hold values from -0.25 to 0.25
- green_mask: int32 [2, 4, 4], replicated, may hold values 0 or 1
- chi_mask: int32 [4, 4], P('row'), may hold values 0 or 1
Outputs:
- chi_blocks: float32 [512, 512], P(('row', 'col'))
Inputs may be any that keep to these rules, and one draw needn't show every extreme that they name: `block_pairs`: in each row exactly 10 slots name basis-pair blocks, all different, and all other slots are -1; in every row, all 2 slots of some col index are named.
All inputs are finite; a program needn't handle non-finite values. No bound on the sum of `chi_mask` on one device may be relied on, other than what follows from the above.
Results may differ from a plain program's by a relative error of at most 0.0041.
Values may be sent and summed in bfloat16 or wider, within the bound.
A program may use at most 128 MiB of HBM per device.

v0:
```python
import jax
import jax.numpy as jnp
from jax import lax
from jax.sharding import PartitionSpec as P

B = 128
AB = 128
NBLK = 4
NNZ = 10


def on_device(x_slots, block_pairs, greens, green_mask, chi_mask):
    row_count = lax.axis_size("row")
    col_count = lax.axis_size("col")
    dev_count = row_count * col_count
    basis_count = NBLK * B
    pair_total = NBLK * NBLK
    row_index = lax.axis_index("row")
    arrived = lax.all_to_all(x_slots[0], "col", split_axis=1, concat_axis=0, tiled=True)
    aux_local = arrived.shape[1]
    pair_list = lax.dynamic_index_in_dim(block_pairs, row_index, 0, keepdims=False)
    selector = (pair_list[:, None] == jnp.arange(pair_total, dtype=jnp.int32)[None, :]).astype(
        jnp.bfloat16
    )
    pair_blocks = jnp.einsum(
        "kq,kabc->qabc", selector, arrived, preferred_element_type=jnp.float32
    ).astype(jnp.bfloat16)
    dense_x = pair_blocks.reshape(NBLK, NBLK, aux_local, B, B).transpose(2, 0, 3, 1, 4)
    dense_x = dense_x.reshape(aux_local, basis_count, basis_count)
    full_mask = jnp.repeat(jnp.repeat(green_mask, B, axis=1), B, axis=2).astype(jnp.bfloat16)
    masked = greens * full_mask
    half_done = jnp.einsum(
        "ml,pmn->pln", masked[0], dense_x, preferred_element_type=jnp.float32
    ).astype(jnp.bfloat16)
    contracted = jnp.einsum(
        "pln,ns->pls", half_done, masked[1], preferred_element_type=jnp.float32
    ).astype(jnp.bfloat16)
    aux_total = dev_count * aux_local
    named_flag = (block_pairs >= 0).astype(jnp.int32)
    position = jnp.cumsum(named_flag, axis=1) - 1
    compact_hit = (position[:, None, :] == jnp.arange(NNZ, dtype=jnp.int32)[None, :, None]) & (
        named_flag[:, None, :] > 0
    )
    compact_sel = compact_hit.astype(jnp.int32)
    named_pairs = jnp.sum(compact_sel * block_pairs[:, None, :], axis=2)
    own_sel = lax.dynamic_index_in_dim(compact_sel, row_index, 0, keepdims=False).astype(
        jnp.bfloat16
    )
    block_span = B * B // dev_count
    x_compact = jnp.einsum(
        "js,sabc->ajbc", own_sel, arrived, preferred_element_type=jnp.float32
    ).astype(jnp.bfloat16)
    x_compact = x_compact.reshape(aux_local, NNZ, dev_count, block_span)
    image_blocks = contracted.reshape(aux_local, NBLK, B, NBLK, B).transpose(0, 1, 3, 2, 4)
    image_blocks = image_blocks.reshape(aux_local, pair_total, dev_count, block_span)
    image_rows, compact_rows = (
        lax.all_to_all(image_blocks, ("row", "col"), split_axis=2, concat_axis=0, tiled=True),
        lax.all_to_all(x_compact, ("row", "col"), split_axis=2, concat_axis=0, tiled=True),
    )
    expand = (
        named_pairs[:, :, None] == jnp.arange(pair_total, dtype=jnp.int32)[None, None, :]
    ).astype(jnp.bfloat16)
    compact_rows = compact_rows.reshape(row_count, aux_total // row_count, NNZ, block_span)
    dense_rows = jnp.einsum(
        "rjk,rqjz->rqkz", expand, compact_rows, preferred_element_type=jnp.float32
    ).astype(jnp.bfloat16)
    image_rows = image_rows.reshape(aux_total, pair_total * block_span)
    dense_rows = dense_rows.reshape(aux_total, pair_total * block_span)
    chi_rows = lax.psum_scatter(
        lax.dot_general(
            image_rows, dense_rows, (((1,), (1,)), ((), ())), preferred_element_type=jnp.float32
        ),
        ("row", "col"),
        scatter_dimension=0,
        tiled=True,
    )
    column_mask = jnp.repeat(chi_mask[0], AB).astype(jnp.float32)
    return chi_rows * column_mask[None, :]


def solution(mesh):
    in_specs = (P("row", "col", None, None, None), P(), P(), P(), P("row", None))
    out_specs = P(("row", "col"), None)
    return jax.shard_map(
        on_device, mesh=mesh, in_specs=in_specs, out_specs=out_specs, check_vma=False
    )
```

profile of v0, /device:TPU:0, one launch (start us, length us, event | category | flops | bytes accessed | tf_op | source)
XLA Modules:
  0.0 733.3 jit_solution(7441425587577253234)
XLA Ops:
  6.5 10.3 %copy.44 = bf16[1,2,128,128,128]{4,3,1,2,0:T(8,128)(2,1)} copy(bf16[1,2,128,128,128]{4,3,2,1,0:T(8,128)(2,1)} %param.5) | data formatting | bytes 16777216 | tf_op args[0]
  16.9 7.4 %all-to-all-start = ((bf16[2,128,128,128]{3,2,0,1:T(8,128)(2,1)}), bf16[2,128,128,128]{3,2,0,1:T(8,128)(2,1)}, u32[]{:S(2)}, u32[]{:S(2)}) async-start(bf16[2,128,128,128]{3,2,0,1:T(8,128)(2,1)} %bitcast.84), calls=%async_computation | async-start | bytes 16777216 | tf_op jit(solution)/shard_map/all_to_all | solution.py:19
  24.5 182.9 %all-to-all-done = bf16[2,128,128,128]{3,2,0,1:T(8,128)(2,1)} async-done(((bf16[2,128,128,128]{3,2,0,1:T(8,128)(2,1)}), bf16[2,128,128,128]{3,2,0,1:T(8,128)(2,1)}, u32[]{:S(2)}, u32[]{:S(2)}) %all-to-all-start) | async-done | bytes 8388640 | tf_op jit(solution)/shard_map/all_to_all | solution.py:19
  207.4 15.6 %copy.23 = bf16[2,8,16,128,128]{4,0,1,3,2:T(2,128)(2,1)S(1)} copy(bf16[2,8,16,128,128]{4,3,0,2,1:T(8,128)(2,1)} %bitcast.4) | data formatting | bytes 16777216 | tf_op jit(solution)/shard_map/all_to_all | solution.py:19
  223.0 3.2 copy-done
  226.2 2.3 convert_bitcast_fusion
  228.6 3.9 copy.29
  232.4 9.2 %reshape.57 = bf16[16,10,32,512]{3,2,1,0:T(8,128)(2,1)} reshape(bf16[16,10,128,128]{3,2,1,0:T(8,128)(2,1)} %copy.29) | data formatting | bytes 10485760 | tf_op jit(solution)/shard_map/reshape | solution.py:53
  241.6 7.7 %copy.30 = bf16[16,10,32,512]{3,0,1,2:T(8,128)(2,1)} copy(bf16[16,10,32,512]{3,2,1,0:T(8,128)(2,1)} %reshape.57) | data formatting | bytes 10485760 | tf_op jit(solution)/shard_map/reshape | solution.py:53
  249.4 4.0 all-to-all-start.2
  253.5 1.6 broadcast_in_dim.7
  255.1 0.4 convert_element_type.66
  255.6 0.3 mul.19
  255.9 5.7 convolution_convert_fusion
  261.6 5.9 copy.43
  267.5 13.1 %reshape.53 = bf16[16,512,512]{2,1,0:T(8,128)(2,1)} reshape(bf16[16,4,128,4,128]{4,3,2,1,0:T(4,128)(2,1)} %bitcast.85) | data formatting | bytes 16777216 | tf_op jit(solution)/shard_map/reshape | solution.py:29
  280.6 13.3 %fusion.3 = bf16[16,512,512]{2,1,0:T(8,128)(2,1)} fusion(bf16[16,512,512]{2,1,0:T(8,128)(2,1)} %reshape.53, bf16[2,512,512]{2,1,0:T(8,128)(2,1)S(1)} %mul.19), kind=kOutput, calls=%fused_computation.7 | convolution fusion | flops 8598323200 | bytes 17825792 | tf_op jit(solution)/shard_map/pln,ns->pls/dot_general | solution.py:35
  293.9 12.6 %reshape.54 = bf16[16,4,128,4,128]{4,3,2,1,0:T(4,128)(2,1)} reshape(bf16[16,512,512]{2,1,0:T(8,128)(2,1)} %fusion.3) | data formatting | bytes 16777216 | tf_op jit(solution)/shard_map/reshape | solution.py:54
  306.4 9.1 %copy.42 = bf16[16,4,128,4,128]{4,2,3,1,0:T(8,128)(2,1)} copy(bf16[16,4,128,4,128]{4,3,2,1,0:T(4,128)(2,1)} %reshape.54) | data formatting | bytes 16777216 | tf_op jit(solution)/shard_map/reshape | solution.py:54
  315.5 13.9 %reshape.55 = bf16[16,16,32,512]{3,2,1,0:T(8,128)(2,1)} reshape(bf16[16,4,4,128,128]{4,3,2,1,0:T(8,128)(2,1)} %bitcast.86) | data formatting | bytes 16777216 | tf_op jit(solution)/shard_map/reshape | solution.py:55
  329.4 11.3 %copy.28 = bf16[16,16,32,512]{3,1,0,2:T(8,128)(2,1)} copy(bf16[16,16,32,512]{3,2,1,0:T(8,128)(2,1)} %reshape.55) | data formatting | bytes 16777216 | tf_op jit(solution)/shard_map/reshape | solution.py:55
  340.8 30.3 %all-to-all-done.2 = bf16[16,10,32,512]{3,0,1,2:T(8,128)(2,1)} async-done(((bf16[16,10,32,512]{3,0,1,2:T(8,128)(2,1)}), bf16[16,10,32,512]{3,0,1,2:T(8,128)(2,1)}, u32[]{:S(2)}, u32[]{:S(2)}) %all-to-all-start.2) | async-done | bytes 5242912 | tf_op jit(solution)/shard_map/all_to_all | solution.py:58
  371.0 3.7 all-to-all-start.1
  374.8 8.8 %reduce-scatter.2.cloned.1.call-start = ((), (), s32[]{:S(2)}) async-start(), calls=%async_computation.4 | async-start | bytes 1081344 | tf_op jit(solution)/shard_map/reduce_scatter | solution.py:69
  383.7 10.9 %copy.31 = bf16[32,16,10,1,512]{4,2,1,0,3:T(8,128)(2,1)} copy(bf16[32,16,10,1,512]{4,1,2,0,3:T(8,128)(2,1)} %bitcast.24) | data formatting | bytes 10485760 | tf_op jit(solution)/shard_map/all_to_all | solution.py:58
  394.6 8.9 %convolution_convert_fusion.1 = bf16[4,128,512,16]{2,3,1,0:T(8,128)(2,1)} fusion(bf16[4,128,10,512]{3,2,1,0:T(8,128)(2,1)} %bitcast.81, s32[4,10]{1,0:T(4,128)S(1)} %select_reduce_fusion), kind=kOutput, calls=%fused_computation.9 | convolution fusion | flops 88081024 | bytes 13631648 | tf_op jit(solution)/shard_map/rjk,rqjz->rqkz/dot_general | solution.py:64
  403.5 16.6 %copy.38 = bf16[64,8,16,512]{3,1,2,0:T(8,128)(2,1)} copy(bf16[64,8,16,512]{3,2,1,0:T(8,128)(2,1)} %bitcast.82) | data formatting | bytes 16777216
  420.1 140.5 %all-to-all-done.1 = bf16[16,16,32,512]{3,1,0,2:T(8,128)(2,1)} async-done(((bf16[16,16,32,512]{3,1,0,2:T(8,128)(2,1)}), bf16[16,16,32,512]{3,1,0,2:T(8,128)(2,1)}, u32[]{:S(2)}, u32[]{:S(2)}) %all-to-all-start.1) | async-done | bytes 8388640 | tf_op jit(solution)/shard_map/all_to_all | solution.py:57
  560.6 16.6 %copy.37 = bf16[64,8,16,512]{3,1,2,0:T(8,128)(2,1)} copy(bf16[64,8,16,512]{3,2,1,0:T(8,128)(2,1)} %bitcast.40) | data formatting | bytes 16777216
  577.2 11.3 %fusion.18 = f32[512,512]{1,0:T(8,128)} fusion(bf16[512,8192]{1,0:T(8,128)(2,1)} %bitcast.88, bf16[512,8192]{1,0:T(8,128)(2,1)} %bitcast.87), kind=kOutput, calls=%fused_computation.32 | convolution fusion | flops 4294967296 | bytes 17825792 | tf_op jit(solution)/shard_map/dot_general | solution.py:70
  588.7 136.0 %reduce-scatter.2.cloned.1.call-done = f32[16,512]{1,0:T(8,128)} async-done(((f32[512,512]{1,0:T(8,128)}), f32[16,512]{1,0:T(8,128)}) %reduce-scatter.2.cloned.1.call-update) | async-done | bytes 32784 | tf_op jit(solution)/shard_map/reduce_scatter | solution.py:69
  724.6 1.4 broadcast_multiply_fusion
  (20 shorter events, 0.5 us)
Async XLA Ops:
  16.9 7.4 %copy-start.2 = (s32[4,16]{1,0:T(4,128)S(1)}, s32[4,16]{1,0:T(4,128)}, u32[]{:S(2)}) copy-start(s32[4,16]{1,0:T(4,128)} %param.6) | copy-start | bytes 772
  16.9 190.6 %all-to-all-start = ((bf16[2,128,128,128]{3,2,0,1:T(8,128)(2,1)}), bf16[2,128,128,128]{3,2,0,1:T(8,128)(2,1)}, u32[]{:S(2)}, u32[]{:S(2)}) async-start(bf16[2,128,128,128]{3,2,0,1:T(8,128)(2,1)} %bitcast.84), calls=%async_computation | async-start | bytes 16777216 | tf_op jit(solution)/shard_map/all_to_all | solution.py:19
  223.0 3.2 copy-start
  241.6 11.8 %copy-start.3 = (s32[2,4,4]{2,1,0:T(4,128)S(1)}, s32[2,4,4]{2,1,0:T(4,128)}, u32[]{:S(2)}) copy-start(s32[2,4,4]{2,1,0:T(4,128)} %param.8) | copy-start | bytes 388
  249.3 6.2 copy-start.1
  249.4 121.7 %all-to-all-start.2 = ((bf16[16,10,32,512]{3,0,1,2:T(8,128)(2,1)}), bf16[16,10,32,512]{3,0,1,2:T(8,128)(2,1)}, u32[]{:S(2)}, u32[]{:S(2)}) async-start(bf16[16,10,32,512]{3,0,1,2:T(8,128)(2,1)} %copy.30), calls=%async_computation.2 | async-start | bytes 10485760 | tf_op jit(solution)/shard_map/all_to_all | solution.py:58
  371.0 189.5 %all-to-all-start.1 = ((bf16[16,16,32,512]{3,1,0,2:T(8,128)(2,1)}), bf16[16,16,32,512]{3,1,0,2:T(8,128)(2,1)}, u32[]{:S(2)}, u32[]{:S(2)}) async-start(bf16[16,16,32,512]{3,1,0,2:T(8,128)(2,1)} %copy.28), calls=%async_computation.1 | async-start | bytes 16777216 | tf_op jit(solution)/shard_map/all_to_all | solution.py:57
  374.8 349.9 %reduce-scatter.2.cloned.1.call-start = ((), (), s32[]{:S(2)}) async-start(), calls=%async_computation.4 | async-start | bytes 1081344 | tf_op jit(solution)/shard_map/reduce_scatter | solution.py:69
  577.2 11.4 %copy-start.4 = (s32[1,4]{1,0:T(1,128)S(1)}, s32[1,4]{1,0:T(1,128)}, u32[]{:S(2)}) copy-start(s32[1,4]{1,0:T(1,128)} %param.9) | copy-start | bytes 52
Sparse Core Ops, SparseCore 0:
  588.7 135.8 reduce-scatter.1
where the time goes:
time: 743 us; the launch traced here: 733 us
  waiting for transfers between devices  490 us (66%)
  local copies, waits for them, and re-layouts  162 us (22%)
  matrix products  41.6 us (6%)
  starting transfers between devices  23.9 us (3%)
  between operations  14 us (2%)
    all_to_all x1, waiting for transfers between devices, on_device(): lax.all_to_all(x_slots[0], 'col', split_axis=1, concat_axis=0, tiled=True)  183 us
    all_to_all x1, waiting for transfers between devices, on_device(): lax.all_to_all(image_blocks, ('row', 'col'), split_axis=2, concat_axis=0,...  140 us
    reduce_scatter x1, waiting for transfers between devices, on_device(): lax.psum_scatter(lax.dot_general(image_rows, dense_rows, (((1,), (1,)), (...  136 us
    unnamed x13, local copies, waits for them, and re-layouts  46.8 us
    all_to_all x1, waiting for transfers between devices, on_device(): lax.all_to_all(x_compact, ('row', 'col'), split_axis=2, concat_axis=0, ti...  30.3 us
    reshape x2, local copies, waits for them, and re-layouts, on_device(): image_blocks.reshape(aux_local, pair_total, dev_count, block_span)  25.3 us
    reshape x2, local copies, waits for them, and re-layouts, on_device(): contracted.reshape(aux_local, NBLK, B, NBLK, B).transpose(0, 1, 3, 2, 4)  21.6 us
    reshape x2, local copies, waits for them, and re-layouts, on_device(): x_compact = x_compact.reshape(aux_local, NNZ, dev_count, block_span)  16.9 us
  transfers between devices with their start and end apart: 4, of which 4 were waited for; matrix products, arithmetic and copies ran while one was open for 17% of the time, Pallas kernels for 0%

commit v1 on v0

--- a/solution.py
+++ b/solution.py
@@ -37,7 +37,9 @@
     ).astype(jnp.bfloat16)
     aux_total = dev_count * aux_local
     named_flag = (block_pairs >= 0).astype(jnp.int32)
-    position = jnp.cumsum(named_flag, axis=1) - 1
+    slot_index = jnp.arange(named_flag.shape[1], dtype=jnp.int32)
+    not_later = (slot_index[None, :] <= slot_index[:, None]).astype(jnp.int32)
+    position = jnp.sum(named_flag[:, None, :] * not_later[None, :, :], axis=2) - 1
     compact_hit = (position[:, None, :] == jnp.arange(NNZ, dtype=jnp.int32)[None, :, None]) & (
         named_flag[:, None, :] > 0
     )
@@ -66,14 +68,17 @@
     ).astype(jnp.bfloat16)
     image_rows = image_rows.reshape(aux_total, pair_total * block_span)
     dense_rows = dense_rows.reshape(aux_total, pair_total * block_span)
-    chi_rows = lax.psum_scatter(
-        lax.dot_general(
-            image_rows, dense_rows, (((1,), (1,)), ((), ())), preferred_element_type=jnp.float32
-        ),
+    chi_part = lax.dot_general(
+        image_rows, dense_rows, (((1,), (1,)), ((), ())), preferred_element_type=jnp.float32
+    )
+    chi_parts = lax.all_to_all(
+        chi_part.reshape(dev_count, aux_local, aux_total),
         ("row", "col"),
-        scatter_dimension=0,
+        split_axis=0,
+        concat_axis=0,
         tiled=True,
     )
+    chi_rows = jnp.sum(chi_parts, axis=0)
     column_mask = jnp.repeat(chi_mask[0], AB).astype(jnp.float32)
     return chi_rows * column_mask[None, :]
 

time: 743 us -> 623 us (0.84)
  waiting for transfers between devices: 490 us -> 393 us
  between operations: 14 us -> 0.64 us
    reduce_scatter x1 -> x0, waiting for transfers between devices: 136 us -> none  [on_device(): lax.psum_scatter(lax.dot_general(image_rows, dense_rows, (((1,), (1,)), (...]
    unnamed x13 -> x11, local copies, waits for them, and re-layouts: 46.8 us -> 13.6 us
    all_to_all x0 -> x1, waiting for transfers between devices: none -> 27.5 us  [on_device(): lax.all_to_all(chi_part.reshape(dev_count, aux_local, aux_total), ('row',...]
    dot_general x0 -> x1, local copies, waits for them, and re-layouts: none -> 13.7 us  [on_device(): lax.dot_general(image_rows, dense_rows, (((1,), (1,)), ((), ())), preferr...]
    reshape x0 -> x1, local copies, waits for them, and re-layouts: none -> 13.5 us  [on_device(): dense_rows = dense_rows.reshape(aux_total, pair_total * block_span)]
    all_to_all x1, waiting for transfers between devices: 140 us -> 152 us  [on_device(): lax.all_to_all(image_blocks, ('row', 'col'), split_axis=2, concat_axis=0,...]
    reduce_scatter x1 -> x0, starting transfers between devices: 8.79 us -> none  [on_device(): lax.psum_scatter(lax.dot_general(image_rows, dense_rows, (((1,), (1,)), (...]
  transfers between devices with their start and end apart: 4 -> 4, of which waited for: 4 -> 4; matrix products, arithmetic and copies ran while one was open for 17% -> 20% of each run, Pallas kernels for 0% -> 0%
where the time goes in v1:
time: 623 us; the launch traced here: 613 us
  waiting for transfers between devices  393 us (63%)
  local copies, waits for them, and re-layouts  156 us (25%)
  matrix products  41.5 us (7%)
  starting transfers between devices  20.6 us (3%)
    all_to_all x1, waiting for transfers between devices, on_device(): lax.all_to_all(x_slots[0], 'col', split_axis=1, concat_axis=0, tiled=True)  183 us
    all_to_all x1, waiting for transfers between devices, on_device(): lax.all_to_all(image_blocks, ('row', 'col'), split_axis=2, concat_axis=0,...  152 us
    all_to_all x1, waiting for transfers between devices, on_device(): lax.all_to_all(x_compact, ('row', 'col'), split_axis=2, concat_axis=0, ti...  30.1 us
    all_to_all x1, waiting for transfers between devices, on_device(): lax.all_to_all(chi_part.reshape(dev_count, aux_local, aux_total), ('row',...  27.5 us
    reshape x2, local copies, waits for them, and re-layouts, on_device(): image_blocks.reshape(aux_local, pair_total, dev_count, block_span)  25.5 us
    reshape x2, local copies, waits for them, and re-layouts, on_device(): contracted.reshape(aux_local, NBLK, B, NBLK, B).transpose(0, 1, 3, 2, 4)  21.6 us
    reshape x2, local copies, waits for them, and re-layouts, on_device(): x_compact = x_compact.reshape(aux_local, NNZ, dev_count, block_span)  16.9 us
    all_to_all x1, local copies, waits for them, and re-layouts, on_device(): lax.all_to_all(x_slots[0], 'col', split_axis=1, concat_axis=0, tiled=True)  15.6 us
  transfers between devices with their start and end apart: 4, of which 4 were waited for; matrix products, arithmetic and copies ran while one was open for 20% of the time, Pallas kernels for 0%

profile of v1, /device:TPU:0, one launch (start us, length us, event | category | flops | bytes accessed | tf_op | source)
XLA Modules:
  0.0 613.3 jit_solution(3637370950011181140)
XLA Ops:
  0.0 10.3 %copy.52 = bf16[1,2,128,128,128]{4,3,1,2,0:T(8,128)(2,1)} copy(bf16[1,2,128,128,128]{4,3,2,1,0:T(8,128)(2,1)} %param.5) | data formatting | bytes 16777216 | tf_op args[0]
  10.3 7.4 %all-to-all-start = ((bf16[2,128,128,128]{3,2,0,1:T(8,128)(2,1)}), bf16[2,128,128,128]{3,2,0,1:T(8,128)(2,1)}, u32[]{:S(2)}, u32[]{:S(2)}) async-start(bf16[2,128,128,128]{3,2,0,1:T(8,128)(2,1)} %bitcast.83), calls=%async_computation | async-start | bytes 16777216 | tf_op jit(solution)/shard_map/all_to_all | solution.py:19
  17.9 183.0 %all-to-all-done = bf16[2,128,128,128]{3,2,0,1:T(8,128)(2,1)} async-done(((bf16[2,128,128,128]{3,2,0,1:T(8,128)(2,1)}), bf16[2,128,128,128]{3,2,0,1:T(8,128)(2,1)}, u32[]{:S(2)}, u32[]{:S(2)}) %all-to-all-start) | async-done | bytes 8388640 | tf_op jit(solution)/shard_map/all_to_all | solution.py:19
  200.9 15.6 %copy.33 = bf16[2,8,16,128,128]{4,0,1,3,2:T(2,128)(2,1)S(1)} copy(bf16[2,8,16,128,128]{4,3,0,2,1:T(8,128)(2,1)} %bitcast.4) | data formatting | bytes 16777216 | tf_op jit(solution)/shard_map/all_to_all | solution.py:19
  216.5 3.2 copy-done
  219.7 2.3 convert_bitcast_fusion.1
  222.0 3.9 copy.39
  225.9 9.2 %reshape.67 = bf16[16,10,32,512]{3,2,1,0:T(8,128)(2,1)} reshape(bf16[16,10,128,128]{3,2,1,0:T(8,128)(2,1)} %copy.39) | data formatting | bytes 10485760 | tf_op jit(solution)/shard_map/reshape | solution.py:55
  235.1 7.7 %copy.40 = bf16[16,10,32,512]{3,0,1,2:T(8,128)(2,1)} copy(bf16[16,10,32,512]{3,2,1,0:T(8,128)(2,1)} %reshape.67) | data formatting | bytes 10485760 | tf_op jit(solution)/shard_map/reshape | solution.py:55
  242.8 4.0 all-to-all-start.2
  246.8 1.6 broadcast_in_dim.7
  248.5 0.4 convert_element_type.73
  248.9 0.3 mul.32
  249.2 5.7 convolution_convert_fusion
  254.9 5.9 copy.51
  260.8 13.1 %reshape.64 = bf16[16,512,512]{2,1,0:T(8,128)(2,1)} reshape(bf16[16,4,128,4,128]{4,3,2,1,0:T(4,128)(2,1)} %bitcast.84) | data formatting | bytes 16777216 | tf_op jit(solution)/shard_map/reshape | solution.py:29
  273.9 13.3 %fusion.3 = bf16[16,512,512]{2,1,0:T(8,128)(2,1)} fusion(bf16[16,512,512]{2,1,0:T(8,128)(2,1)} %reshape.64, bf16[2,512,512]{2,1,0:T(8,128)(2,1)S(1)} %mul.32), kind=kOutput, calls=%fused_computation.8 | convolution fusion | flops 8598323200 | bytes 17825792 | tf_op jit(solution)/shard_map/pln,ns->pls/dot_general | solution.py:35
  287.2 12.5 %reshape.65 = bf16[16,4,128,4,128]{4,3,2,1,0:T(4,128)(2,1)} reshape(bf16[16,512,512]{2,1,0:T(8,128)(2,1)} %fusion.3) | data formatting | bytes 16777216 | tf_op jit(solution)/shard_map/reshape | solution.py:56
  299.7 9.0 %copy.50 = bf16[16,4,128,4,128]{4,2,3,1,0:T(8,128)(2,1)} copy(bf16[16,4,128,4,128]{4,3,2,1,0:T(4,128)(2,1)} %reshape.65) | data formatting | bytes 16777216 | tf_op jit(solution)/shard_map/reshape | solution.py:56
  308.8 14.1 %reshape.66 = bf16[16,16,32,512]{3,2,1,0:T(8,128)(2,1)} reshape(bf16[16,4,4,128,128]{4,3,2,1,0:T(8,128)(2,1)} %bitcast.85) | data formatting | bytes 16777216 | tf_op jit(solution)/shard_map/reshape | solution.py:57
  322.9 11.3 %copy.38 = bf16[16,16,32,512]{3,1,0,2:T(8,128)(2,1)} copy(bf16[16,16,32,512]{3,2,1,0:T(8,128)(2,1)} %reshape.66) | data formatting | bytes 16777216 | tf_op jit(solution)/shard_map/reshape | solution.py:57
  334.3 30.1 %all-to-all-done.2 = bf16[16,10,32,512]{3,0,1,2:T(8,128)(2,1)} async-done(((bf16[16,10,32,512]{3,0,1,2:T(8,128)(2,1)}), bf16[16,10,32,512]{3,0,1,2:T(8,128)(2,1)}, u32[]{:S(2)}, u32[]{:S(2)}) %all-to-all-start.2) | async-done | bytes 5242912 | tf_op jit(solution)/shard_map/all_to_all | solution.py:60
  364.4 3.7 all-to-all-start.1
  368.2 10.9 %copy.41 = bf16[32,16,10,1,512]{4,2,1,0,3:T(8,128)(2,1)} copy(bf16[32,16,10,1,512]{4,1,2,0,3:T(8,128)(2,1)} %bitcast.24) | data formatting | bytes 10485760 | tf_op jit(solution)/shard_map/all_to_all | solution.py:60
  379.1 8.9 %convert_bitcast_fusion = bf16[4,128,16,512]{3,2,1,0:T(8,128)(2,1)} fusion(bf16[4,128,10,512]{3,2,1,0:T(8,128)(2,1)} %bitcast.81, s32[4,10]{1,0:T(4,128)S(1)} %select_reduce_fusion), kind=kOutput, calls=%fused_computation.5 | convolution fusion | flops 88081024 | bytes 13631648 | tf_op jit(solution)/shard_map/rjk,rqjz->rqkz/dot_general | solution.py:66
  388.0 13.5 %reshape.75 = bf16[512,8192,1]{1,0,2:T(8,128)(2,1)} reshape(bf16[4,128,16,512]{3,2,1,0:T(8,128)(2,1)} %convert_bitcast_fusion) | data formatting | bytes 16777216 | tf_op jit(solution)/shard_map/reshape | solution.py:70
  401.5 152.4 %all-to-all-done.1 = bf16[16,16,32,512]{3,1,0,2:T(8,128)(2,1)} async-done(((bf16[16,16,32,512]{3,1,0,2:T(8,128)(2,1)}), bf16[16,16,32,512]{3,1,0,2:T(8,128)(2,1)}, u32[]{:S(2)}, u32[]{:S(2)}) %all-to-all-start.1) | async-done | bytes 8388640 | tf_op jit(solution)/shard_map/all_to_all | solution.py:59
  553.9 13.7 %dot_general.23 = bf16[32,16,8192]{2,1,0:T(8,128)(2,1)} reshape(bf16[32,16,16,1,512]{4,2,1,0,3:T(8,128)(2,1)} %bitcast.17) | data formatting | bytes 16777216 | tf_op jit(solution)/shard_map/dot_general | solution.py:71
  567.7 11.3 %fusion.19 = f32[32,16,512]{2,1,0:T(8,128)} fusion(bf16[32,16,8192]{2,1,0:T(8,128)(2,1)} %dot_general.23, bf16[512,8192,1]{1,0,2:T(8,128)(2,1)} %reshape.75), kind=kOutput, calls=%fused_computation.35 | convolution fusion | flops 4294967296 | bytes 17825792 | tf_op jit(solution)/shard_map/dot_general | solution.py:71
  579.0 5.5 all-to-all-start.3
  584.6 27.5 %all-to-all-done.3 = f32[32,16,512]{2,1,0:T(8,128)S(1)} async-done(((f32[32,16,512]{2,1,0:T(8,128)}), f32[32,16,512]{2,1,0:T(8,128)S(1)}, u32[]{:S(2)}, u32[]{:S(2)}) %all-to-all-start.3) | async-done | bytes 1048608 | tf_op jit(solution)/shard_map/all_to_all | solution.py:74
  612.2 0.6 broadcast_multiply_fusion
  (21 shorter events, 0.5 us)
Async XLA Ops:
  10.3 7.4 %copy-start.2 = (s32[4,16]{1,0:T(4,128)S(1)}, s32[4,16]{1,0:T(4,128)}, u32[]{:S(2)}) copy-start(s32[4,16]{1,0:T(4,128)} %param.6) | copy-start | bytes 772
  10.3 190.6 %all-to-all-start = ((bf16[2,128,128,128]{3,2,0,1:T(8,128)(2,1)}), bf16[2,128,128,128]{3,2,0,1:T(8,128)(2,1)}, u32[]{:S(2)}, u32[]{:S(2)}) async-start(bf16[2,128,128,128]{3,2,0,1:T(8,128)(2,1)} %bitcast.83), calls=%async_computation | async-start | bytes 16777216 | tf_op jit(solution)/shard_map/all_to_all | solution.py:19
  216.5 3.2 copy-start
  235.1 11.7 %copy-start.3 = (s32[2,4,4]{2,1,0:T(4,128)S(1)}, s32[2,4,4]{2,1,0:T(4,128)}, u32[]{:S(2)}) copy-start(s32[2,4,4]{2,1,0:T(4,128)} %param.8) | copy-start | bytes 388
  242.8 6.1 copy-start.1
  242.8 121.6 %all-to-all-start.2 = ((bf16[16,10,32,512]{3,0,1,2:T(8,128)(2,1)}), bf16[16,10,32,512]{3,0,1,2:T(8,128)(2,1)}, u32[]{:S(2)}, u32[]{:S(2)}) async-start(bf16[16,10,32,512]{3,0,1,2:T(8,128)(2,1)} %copy.40), calls=%async_computation.2 | async-start | bytes 10485760 | tf_op jit(solution)/shard_map/all_to_all | solution.py:60
  364.4 189.5 %all-to-all-start.1 = ((bf16[16,16,32,512]{3,1,0,2:T(8,128)(2,1)}), bf16[16,16,32,512]{3,1,0,2:T(8,128)(2,1)}, u32[]{:S(2)}, u32[]{:S(2)}) async-start(bf16[16,16,32,512]{3,1,0,2:T(8,128)(2,1)} %copy.38), calls=%async_computation.1 | async-start | bytes 16777216 | tf_op jit(solution)/shard_map/all_to_all | solution.py:59
  567.7 16.9 %copy-start.4 = (s32[1,4]{1,0:T(1,128)S(1)}, s32[1,4]{1,0:T(1,128)}, u32[]{:S(2)}) copy-start(s32[1,4]{1,0:T(1,128)} %param.9) | copy-start | bytes 52
  579.0 33.1 %all-to-all-start.3 = ((f32[32,16,512]{2,1,0:T(8,128)}), f32[32,16,512]{2,1,0:T(8,128)S(1)}, u32[]{:S(2)}, u32[]{:S(2)}) async-start(f32[32,16,512]{2,1,0:T(8,128)} %fusion.19), calls=%async_computation.3 | async-start | bytes 2097152 | tf_op jit(solution)/shard_map/all_to_all | solution.py:74

commit v2 on v1

v2 whole, which is shorter than its diff:
```python
import jax
import jax.numpy as jnp
from jax import lax
from jax.sharding import PartitionSpec as P

B = 128
AB = 128
NBLK = 4
NNZ = 10
CHUNKS = 2


def on_device(x_slots, block_pairs, greens, green_mask, chi_mask):
    row_count = lax.axis_size("row")
    col_count = lax.axis_size("col")
    dev_count = row_count * col_count
    basis_count = NBLK * B
    pair_total = NBLK * NBLK
    row_index = lax.axis_index("row")
    slots = x_slots[0]
    chunk = slots.shape[1] // (col_count * CHUNKS)
    grouped = slots.reshape(slots.shape[0], col_count, CHUNKS, chunk, B, B)
    arrivals = [
        lax.all_to_all(
            grouped[:, :, part].reshape(slots.shape[0], col_count * chunk, B, B),
            "col",
            split_axis=1,
            concat_axis=0,
            tiled=True,
        )
        for part in range(CHUNKS)
    ]
    aux_local = chunk * CHUNKS
    pair_list = lax.dynamic_index_in_dim(block_pairs, row_index, 0, keepdims=False)
    selector = (pair_list[:, None] == jnp.arange(pair_total, dtype=jnp.int32)[None, :]).astype(
        jnp.bfloat16
    )
    full_mask = jnp.repeat(jnp.repeat(green_mask, B, axis=1), B, axis=2).astype(jnp.bfloat16)
    masked = greens * full_mask
    aux_total = dev_count * aux_local
    named_flag = (block_pairs >= 0).astype(jnp.int32)
    slot_index = jnp.arange(named_flag.shape[1], dtype=jnp.int32)
    not_later = (slot_index[None, :] <= slot_index[:, None]).astype(jnp.int32)
    position = jnp.sum(named_flag[:, None, :] * not_later[None, :, :], axis=2) - 1
    compact_hit = (position[:, None, :] == jnp.arange(NNZ, dtype=jnp.int32)[None, :, None]) & (
        named_flag[:, None, :] > 0
    )
    compact_sel = compact_hit.astype(jnp.int32)
    named_pairs = jnp.sum(compact_sel * block_pairs[:, None, :], axis=2)
    own_sel = lax.dynamic_index_in_dim(compact_sel, row_index, 0, keepdims=False).astype(
        jnp.bfloat16
    )
    block_span = B * B // dev_count
    expand = (
        named_pairs[:, :, None] == jnp.arange(pair_total, dtype=jnp.int32)[None, None, :]
    ).astype(jnp.bfloat16)
    image_parts, dense_parts = [], []
    for arrived in arrivals:
        x_compact = jnp.einsum(
            "js,sabc->ajbc", own_sel, arrived, preferred_element_type=jnp.float32
        ).astype(jnp.bfloat16)
        x_compact = x_compact.reshape(chunk, NNZ, dev_count, block_span)
        compact_rows = lax.all_to_all(
            x_compact, ("row", "col"), split_axis=2, concat_axis=0, tiled=True
        )
        pair_blocks = jnp.einsum(
            "kq,kabc->qabc", selector, arrived, preferred_element_type=jnp.float32
        ).astype(jnp.bfloat16)
        dense_x = pair_blocks.reshape(NBLK, NBLK, chunk, B, B).transpose(2, 0, 3, 1, 4)
        dense_x = dense_x.reshape(chunk, basis_count, basis_count)
        half_done = jnp.einsum(
            "ml,pmn->pln", masked[0], dense_x, preferred_element_type=jnp.float32
        ).astype(jnp.bfloat16)
        contracted = jnp.einsum(
            "pln,ns->pls", half_done, masked[1], preferred_element_type=jnp.float32
        ).astype(jnp.bfloat16)
        image_blocks = contracted.reshape(chunk, NBLK, B, NBLK, B).transpose(0, 1, 3, 2, 4)
        image_blocks = image_blocks.reshape(chunk, pair_total, dev_count, block_span)
        image_rows = lax.all_to_all(
            image_blocks, ("row", "col"), split_axis=2, concat_axis=0, tiled=True
        )
        compact_rows = compact_rows.reshape(row_count, col_count * chunk, NNZ, block_span)
        dense_rows = jnp.einsum(
            "rjk,rqjz->rqkz", expand, compact_rows, preferred_element_type=jnp.float32
        ).astype(jnp.bfloat16)
        image_rows = image_rows.reshape(dev_count, 1, chunk, pair_total * block_span)
        dense_rows = dense_rows.reshape(dev_count, 1, chunk, pair_total * block_span)
        image_parts.append(image_rows)
        dense_parts.append(dense_rows)
    image_rows = jnp.concatenate(image_parts, axis=1).reshape(aux_total, pair_total * block_span)
    dense_rows = jnp.concatenate(dense_parts, axis=1).reshape(aux_total, pair_total * block_span)
    chi_part = lax.dot_general(
        image_rows, dense_rows, (((1,), (1,)), ((), ())), preferred_element_type=jnp.float32
    )
    chi_parts = lax.all_to_all(
        chi_part.reshape(dev_count, aux_local, aux_total),
        ("row", "col"),
        split_axis=0,
        concat_axis=0,
        tiled=True,
    )
    chi_rows = jnp.sum(chi_parts, axis=0)
    column_mask = jnp.repeat(chi_mask[0], AB).astype(jnp.float32)
    return chi_rows * column_mask[None, :]


def solution(mesh):
    in_specs = (P("row", "col", None, None, None), P(), P(), P(), P("row", None))
    out_specs = P(("row", "col"), None)
    return jax.shard_map(
        on_device, mesh=mesh, in_specs=in_specs, out_specs=out_specs, check_vma=False
    )
```

time: 623 us -> 594 us (0.953)
  waiting for transfers between devices: 393 us -> 330 us
  local copies, waits for them, and re-layouts: 156 us -> 167 us
  other arithmetic: 1.3 us -> 11.3 us
  starting transfers between devices: 20.6 us -> 30.4 us
    all_to_all x1 -> x2, waiting for transfers between devices: 152 us -> 91.7 us  [on_device(): lax.all_to_all(image_blocks, ('row', 'col'), split_axis=2, concat_axis=0,...]
    reshape x9 -> x20, local copies, waits for them, and re-layouts: 96.4 us -> 119 us  [the longest x4 28.1 us: on_device(): image_blocks.reshape(chunk, pair_total, dev_count, block_span)]
    all_to_all x1 -> x2, waiting for transfers between devices: 183 us -> 163 us  [on_device(): lax.all_to_all(grouped[:, :, part].reshape(slots.shape[0], col_count * ch...]
    all_to_all x1 -> x2, waiting for transfers between devices: 30.1 us -> 47.3 us  [on_device(): lax.all_to_all(x_compact, ('row', 'col'), split_axis=2, concat_axis=0, ti...]
    dot_general x1 -> x0, local copies, waits for them, and re-layouts: 13.7 us -> none  [on_device(): lax.dot_general(image_rows, dense_rows, (((1,), (1,)), ((), ())), preferr...]
    concatenate x0 -> x1, local copies, waits for them, and re-layouts: none -> 7.59 us  [on_device(): jnp.concatenate(dense_parts, axis=1)]
    concatenate x0 -> x1, other arithmetic: none -> 7.46 us  [on_device(): jnp.concatenate(dense_parts, axis=1)]
    all_to_all x1 -> x2, local copies, waits for them, and re-layouts: 10.9 us -> 4.65 us  [on_device(): lax.all_to_all(x_compact, ('row', 'col'), split_axis=2, concat_axis=0, ti...]
  transfers between devices with their start and end apart: 4 -> 7, of which waited for: 4 -> 7; matrix products, arithmetic and copies ran while one was open for 20% -> 33% of each run, Pallas kernels for 0% -> 0%
where the time goes in v2:
time: 594 us; the launch traced here: 584 us
  waiting for transfers between devices  330 us (56%)
  local copies, waits for them, and re-layouts  167 us (28%)
  matrix products  45 us (8%)
  starting transfers between devices  30.4 us (5%)
  other arithmetic  11.3 us (2%)
    all_to_all x2, waiting for transfers between devices, on_device(): lax.all_to_all(grouped[:, :, part].reshape(slots.shape[0], col_count * ch...  163 us
    all_to_all x2, waiting for transfers between devices, on_device(): lax.all_to_all(image_blocks, ('row', 'col'), split_axis=2, concat_axis=0,...  91.7 us
    all_to_all x2, waiting for transfers between devices, on_device(): lax.all_to_all(x_compact, ('row', 'col'), split_axis=2, concat_axis=0, ti...  47.3 us
    reshape x4, local copies, waits for them, and re-layouts, on_device(): image_blocks.reshape(chunk, pair_total, dev_count, block_span)  28.1 us
    all_to_all x1, waiting for transfers between devices, on_device(): lax.all_to_all(chi_part.reshape(dev_count, aux_local, aux_total), ('row',...  27.5 us
    reshape x4, local copies, waits for them, and re-layouts, on_device(): contracted.reshape(chunk, NBLK, B, NBLK, B).transpose(0, 1, 3, 2, 4)  24.5 us
    dot_general x2, matrix products, on_device(): jnp.einsum('pln,ns->pls', half_done, masked[1], preferred_element_type=jn...  18 us
    reshape x2, local copies, waits for them, and re-layouts, on_device(): dense_rows.reshape(dev_count, 1, chunk, pair_total * block_span)  14.9 us
  transfers between devices with their start and end apart: 7, of which 7 were waited for; matrix products, arithmetic and copies ran while one was open for 33% of the time, Pallas kernels for 0%

profile of v2, /device:TPU:0, one launch (start us, length us, event | category | flops | bytes accessed | tf_op | source)
XLA Modules:
  0.0 584.1 jit_solution(14850925202088278918)
XLA Ops:
  0.0 5.2 fusion.36
  7.5 7.3 %all-to-all-start = ((bf16[2,64,128,128]{3,2,0,1:T(8,128)(2,1)}), bf16[2,64,128,128]{3,2,0,1:T(8,128)(2,1)}, u32[]{:S(2)}, u32[]{:S(2)}) async-start(bf16[2,64,128,128]{3,2,0,1:T(8,128)(2,1)} %bitcast.136), calls=%async_computation | async-start | bytes 8388608 | tf_op jit(solution)/shard_map/all_to_all | solution.py:24
  14.7 4.7 copy.120
  19.4 88.6 %all-to-all-done = bf16[2,64,128,128]{3,2,0,1:T(8,128)(2,1)} async-done(((bf16[2,64,128,128]{3,2,0,1:T(8,128)(2,1)}), bf16[2,64,128,128]{3,2,0,1:T(8,128)(2,1)}, u32[]{:S(2)}, u32[]{:S(2)}) %all-to-all-start) | async-done | bytes 4194336 | tf_op jit(solution)/shard_map/all_to_all | solution.py:24
  108.0 4.7 all-to-all-start.2
  112.9 6.5 %copy.88 = bf16[8,2,8,128,128]{4,1,0,3,2:T(2,128)(2,1)S(1)} copy(bf16[8,2,8,128,128]{4,3,1,2,0:T(8,128)(2,1)} %bitcast.7) | data formatting | bytes 8388608 | tf_op jit(solution)/shard_map/all_to_all | solution.py:24
  130.7 74.6 %all-to-all-done.2 = bf16[2,64,128,128]{3,2,0,1:T(8,128)(2,1)} async-done(((bf16[2,64,128,128]{3,2,0,1:T(8,128)(2,1)}), bf16[2,64,128,128]{3,2,0,1:T(8,128)(2,1)}, u32[]{:S(2)}, u32[]{:S(2)}) %all-to-all-start.2) | async-done | bytes 4194336 | tf_op jit(solution)/shard_map/all_to_all | solution.py:24
  209.5 6.5 %copy.96 = bf16[8,2,8,128,128]{4,1,0,3,2:T(2,128)(2,1)S(1)} copy(bf16[8,2,8,128,128]{4,3,1,2,0:T(8,128)(2,1)} %bitcast.24) | data formatting | bytes 8388608 | tf_op jit(solution)/shard_map/all_to_all | solution.py:24
  227.4 43.5 %all-to-all-done.4 = bf16[8,10,32,512]{3,0,1,2:T(8,128)(2,1)} async-done(((bf16[8,10,32,512]{3,0,1,2:T(8,128)(2,1)}), bf16[8,10,32,512]{3,0,1,2:T(8,128)(2,1)}, u32[]{:S(2)}, u32[]{:S(2)}) %all-to-all-start.4) | async-done | bytes 2621472 | tf_op jit(solution)/shard_map/all_to_all | solution.py:63
  289.5 7.3 %reshape.97 = bf16[8,512,512]{2,1,0:T(8,128)(2,1)} reshape(bf16[8,4,128,4,128]{4,3,2,1,0:T(4,128)(2,1)} %bitcast.140) | data formatting | bytes 8388608 | tf_op jit(solution)/shard_map/reshape | solution.py:70
  296.7 9.0 %fusion.9 = bf16[8,512,512]{2,1,0:T(8,128)(2,1)} fusion(bf16[8,512,512]{2,1,0:T(8,128)(2,1)} %reshape.97, bf16[2,512,512]{2,1,0:T(8,128)(2,1)} %mul.32), kind=kOutput, calls=%fused_computation.19 | convolution fusion | flops 4299161600 | bytes 9437184 | tf_op jit(solution)/shard_map/pln,ns->pls/dot_general | solution.py:74
  305.7 7.0 %reshape.98 = bf16[8,4,128,4,128]{4,3,2,1,0:T(4,128)(2,1)} reshape(bf16[8,512,512]{2,1,0:T(8,128)(2,1)} %fusion.9) | data formatting | bytes 8388608 | tf_op jit(solution)/shard_map/reshape | solution.py:77
  312.7 5.3 copy.131
  318.0 7.6 %reshape.99 = bf16[8,16,32,512]{3,2,1,0:T(8,128)(2,1)} reshape(bf16[8,4,4,128,128]{4,3,2,1,0:T(8,128)(2,1)} %bitcast.141) | data formatting | bytes 8388608 | tf_op jit(solution)/shard_map/reshape | solution.py:78
  325.6 6.5 %copy.93 = bf16[8,16,32,512]{3,1,0,2:T(8,128)(2,1)} copy(bf16[8,16,32,512]{3,2,1,0:T(8,128)(2,1)} %reshape.99) | data formatting | bytes 8388608 | tf_op jit(solution)/shard_map/reshape | solution.py:78
  343.3 4.3 copy.130
  347.6 7.2 %reshape.102 = bf16[8,512,512]{2,1,0:T(8,128)(2,1)} reshape(bf16[8,4,128,4,128]{4,3,2,1,0:T(4,128)(2,1)} %bitcast.142) | data formatting | bytes 8388608 | tf_op jit(solution)/shard_map/reshape | solution.py:70
  354.7 9.0 %fusion.12 = bf16[8,512,512]{2,1,0:T(8,128)(2,1)} fusion(bf16[8,512,512]{2,1,0:T(8,128)(2,1)} %reshape.102, bf16[2,512,512]{2,1,0:T(8,128)(2,1)} %mul.32), kind=kOutput, calls=%fused_computation.20 | convolution fusion | flops 4299161600 | bytes 9437184 | tf_op jit(solution)/shard_map/pln,ns->pls/dot_general | solution.py:74
  363.7 6.9 %reshape.103 = bf16[8,4,128,4,128]{4,3,2,1,0:T(4,128)(2,1)} reshape(bf16[8,512,512]{2,1,0:T(8,128)(2,1)} %fusion.12) | data formatting | bytes 8388608 | tf_op jit(solution)/shard_map/reshape | solution.py:77
  370.6 5.3 copy.129
  375.9 7.5 %reshape.104 = bf16[8,16,32,512]{3,2,1,0:T(8,128)(2,1)} reshape(bf16[8,4,4,128,128]{4,3,2,1,0:T(8,128)(2,1)} %bitcast.143) | data formatting | bytes 8388608 | tf_op jit(solution)/shard_map/reshape | solution.py:78
  383.5 6.5 %copy.101 = bf16[8,16,32,512]{3,1,0,2:T(8,128)(2,1)} copy(bf16[8,16,32,512]{3,2,1,0:T(8,128)(2,1)} %reshape.104) | data formatting | bytes 8388608 | tf_op jit(solution)/shard_map/reshape | solution.py:78
  390.0 45.0 %all-to-all-done.1 = bf16[8,16,32,512]{3,1,0,2:T(8,128)(2,1)} async-done(((bf16[8,16,32,512]{3,1,0,2:T(8,128)(2,1)}), bf16[8,16,32,512]{3,1,0,2:T(8,128)(2,1)}, u32[]{:S(2)}, u32[]{:S(2)}) %all-to-all-start.1) | async-done | bytes 4194336 | tf_op jit(solution)/shard_map/all_to_all | solution.py:79
  445.4 7.4 %reshape.108 = bf16[32,1,8,8192]{3,2,0,1:T(8,128)(2,1)} reshape(bf16[4,64,16,512]{3,2,1,0:T(8,128)(2,1)} %convert_bitcast_fusion.2) | data formatting | bytes 8388608 | tf_op jit(solution)/shard_map/reshape | solution.py:87
  457.4 7.5 %reshape.111 = bf16[32,1,8,8192]{3,2,0,1:T(8,128)(2,1)} reshape(bf16[4,64,16,512]{3,2,1,0:T(8,128)(2,1)} %convert_bitcast_fusion) | data formatting | bytes 8388608 | tf_op jit(solution)/shard_map/reshape | solution.py:87
  464.9 7.5 %pad_maximum_fusion.1 = bf16[32,2,8,8192]{3,2,0,1:T(8,128)(2,1)} fusion(bf16[32,1,8,8192]{3,2,0,1:T(8,128)(2,1)} %reshape.111, bf16[32,1,8,8192]{3,2,0,1:T(8,128)(2,1)} %reshape.108), kind=kLoop, calls=%fused_computation.1 | loop fusion | flops 4194304 | bytes 16777216 | tf_op jit(solution)/shard_map/concatenate | solution.py:91
  472.3 7.6 %copy.109 = bf16[32,2,8,8192]{3,2,1,0:T(8,128)(2,1)} copy(bf16[32,2,8,8192]{3,2,0,1:T(8,128)(2,1)} %pad_maximum_fusion.1) | data formatting | bytes 16777216 | tf_op jit(solution)/shard_map/concatenate | solution.py:91
  479.9 7.4 %reshape.100 = bf16[32,1,8,8192]{3,2,0,1:T(8,128)(2,1)} reshape(bf16[32,8,16,1,512]{4,2,1,0,3:T(8,128)(2,1)} %bitcast.19) | data formatting | bytes 8388608 | tf_op jit(solution)/shard_map/reshape | solution.py:86
  487.3 46.6 %all-to-all-done.3 = bf16[8,16,32,512]{3,1,0,2:T(8,128)(2,1)} async-done(((bf16[8,16,32,512]{3,1,0,2:T(8,128)(2,1)}), bf16[8,16,32,512]{3,1,0,2:T(8,128)(2,1)}, u32[]{:S(2)}, u32[]{:S(2)}) %all-to-all-start.3) | async-done | bytes 4194336 | tf_op jit(solution)/shard_map/all_to_all | solution.py:79
  534.0 7.4 %reshape.105 = bf16[32,1,8,8192]{3,2,0,1:T(8,128)(2,1)} reshape(bf16[32,8,16,1,512]{4,2,1,0,3:T(8,128)(2,1)} %bitcast.31) | data formatting | bytes 8388608 | tf_op jit(solution)/shard_map/reshape | solution.py:86
  541.4 11.4 %fusion = f32[32,16,512]{2,1,0:T(8,128)} fusion(bf16[512,8192,1]{1,0,2:T(8,128)(2,1)} %bitcast.147, bf16[32,1,8,8192]{3,2,0,1:T(8,128)(2,1)} %reshape.105, bf16[32,1,8,8192]{3,2,0,1:T(8,128)(2,1)} %reshape.100), kind=kOutput, calls=%fused_computation.2 | convolution fusion | flops 4299161600 | bytes 17825792 | tf_op jit(solution)/shard_map/dot_general | solution.py:92
  555.5 27.5 %all-to-all-done.6 = f32[32,16,512]{2,1,0:T(8,128)S(1)} async-done(((f32[32,16,512]{2,1,0:T(8,128)}), f32[32,16,512]{2,1,0:T(8,128)S(1)}, u32[]{:S(2)}, u32[]{:S(2)}) %all-to-all-start.6) | async-done | bytes 1048608 | tf_op jit(solution)/shard_map/all_to_all | solution.py:95
  (48 shorter events, 77.4 us)
Async XLA Ops:
  7.5 100.5 %all-to-all-start = ((bf16[2,64,128,128]{3,2,0,1:T(8,128)(2,1)}), bf16[2,64,128,128]{3,2,0,1:T(8,128)(2,1)}, u32[]{:S(2)}, u32[]{:S(2)}) async-start(bf16[2,64,128,128]{3,2,0,1:T(8,128)(2,1)} %bitcast.136), calls=%async_computation | async-start | bytes 8388608 | tf_op jit(solution)/shard_map/all_to_all | solution.py:24
  108.0 4.7 copy-start.2
  108.0 97.2 %all-to-all-start.2 = ((bf16[2,64,128,128]{3,2,0,1:T(8,128)(2,1)}), bf16[2,64,128,128]{3,2,0,1:T(8,128)(2,1)}, u32[]{:S(2)}, u32[]{:S(2)}) async-start(bf16[2,64,128,128]{3,2,0,1:T(8,128)(2,1)} %bitcast.135), calls=%async_computation.2 | async-start | bytes 8388608 | tf_op jit(solution)/shard_map/all_to_all | solution.py:24
  119.4 2.0 copy-start.1
  205.2 65.6 %all-to-all-start.4 = ((bf16[8,10,32,512]{3,0,1,2:T(8,128)(2,1)}), bf16[8,10,32,512]{3,0,1,2:T(8,128)(2,1)}, u32[]{:S(2)}, u32[]{:S(2)}) async-start(bf16[8,10,32,512]{3,0,1,2:T(8,128)(2,1)} %copy.104), calls=%async_computation.4 | async-start | bytes 5242880 | tf_op jit(solution)/shard_map/all_to_all | solution.py:63
  216.0 2.0 copy-start
  224.4 50.2 %copy-start.3 = (s32[2,4,4]{2,1,0:T(4,128)S(1)}, s32[2,4,4]{2,1,0:T(4,128)}, u32[]{:S(2)}) copy-start(s32[2,4,4]{2,1,0:T(4,128)} %param.8) | copy-start | bytes 388
  270.8 65.1 %all-to-all-start.5 = ((bf16[8,10,32,512]{3,0,1,2:T(8,128)(2,1)}), bf16[8,10,32,512]{3,0,1,2:T(8,128)(2,1)S(1)}, u32[]{:S(2)}, u32[]{:S(2)}) async-start(bf16[8,10,32,512]{3,0,1,2:T(8,128)(2,1)} %copy.107), calls=%async_computation.5 | async-start | bytes 5242880 | tf_op jit(solution)/shard_map/all_to_all | solution.py:63
  335.9 99.1 %all-to-all-start.1 = ((bf16[8,16,32,512]{3,1,0,2:T(8,128)(2,1)}), bf16[8,16,32,512]{3,1,0,2:T(8,128)(2,1)}, u32[]{:S(2)}, u32[]{:S(2)}) async-start(bf16[8,16,32,512]{3,1,0,2:T(8,128)(2,1)} %copy.93), calls=%async_computation.1 | async-start | bytes 8388608 | tf_op jit(solution)/shard_map/all_to_all | solution.py:79
  435.0 99.0 %all-to-all-start.3 = ((bf16[8,16,32,512]{3,1,0,2:T(8,128)(2,1)}), bf16[8,16,32,512]{3,1,0,2:T(8,128)(2,1)}, u32[]{:S(2)}, u32[]{:S(2)}) async-start(bf16[8,16,32,512]{3,1,0,2:T(8,128)(2,1)} %copy.101), calls=%async_computation.3 | async-start | bytes 8388608 | tf_op jit(solution)/shard_map/all_to_all | solution.py:79
  541.4 14.0 %copy-start.4 = (s32[1,4]{1,0:T(1,128)S(1)}, s32[1,4]{1,0:T(1,128)}, u32[]{:S(2)}) copy-start(s32[1,4]{1,0:T(1,128)} %param.9) | copy-start | bytes 52
  552.7 30.2 %all-to-all-start.6 = ((f32[32,16,512]{2,1,0:T(8,128)}), f32[32,16,512]{2,1,0:T(8,128)S(1)}, u32[]{:S(2)}, u32[]{:S(2)}) async-start(f32[32,16,512]{2,1,0:T(8,128)} %fusion), calls=%async_computation.6 | async-start | bytes 2097152 | tf_op jit(solution)/shard_map/all_to_all | solution.py:95

commit v3 on v2

--- a/solution.py
+++ b/solution.py
@@ -87,19 +87,24 @@
         dense_rows = dense_rows.reshape(dev_count, 1, chunk, pair_total * block_span)
         image_parts.append(image_rows)
         dense_parts.append(dense_rows)
-    image_rows = jnp.concatenate(image_parts, axis=1).reshape(aux_total, pair_total * block_span)
     dense_rows = jnp.concatenate(dense_parts, axis=1).reshape(aux_total, pair_total * block_span)
-    chi_part = lax.dot_general(
-        image_rows, dense_rows, (((1,), (1,)), ((), ())), preferred_element_type=jnp.float32
-    )
-    chi_parts = lax.all_to_all(
-        chi_part.reshape(dev_count, aux_local, aux_total),
-        ("row", "col"),
-        split_axis=0,
-        concat_axis=0,
-        tiled=True,
-    )
-    chi_rows = jnp.sum(chi_parts, axis=0)
+    chi_sums = []
+    for image_rows in image_parts:
+        chi_part = lax.dot_general(
+            image_rows.reshape(dev_count * chunk, pair_total * block_span),
+            dense_rows,
+            (((1,), (1,)), ((), ())),
+            preferred_element_type=jnp.float32,
+        )
+        chi_parts = lax.all_to_all(
+            chi_part.reshape(dev_count, chunk, aux_total),
+            ("row", "col"),
+            split_axis=0,
+            concat_axis=0,
+            tiled=True,
+        )
+        chi_sums.append(jnp.sum(chi_parts, axis=0))
+    chi_rows = jnp.concatenate(chi_sums, axis=0)
     column_mask = jnp.repeat(chi_mask[0], AB).astype(jnp.float32)
     return chi_rows * column_mask[None, :]
 

time: 594 us -> 585 us (0.985)
  waiting for transfers between devices: 330 us -> 311 us
    reshape x2 -> x0, local copies, waits for them, and re-layouts: 14.8 us -> none  [on_device(): image_rows.reshape(dev_count, 1, chunk, pair_total * block_span)]
    dot_general x0 -> x2, local copies, waits for them, and re-layouts: none -> 14.8 us  [on_device(): lax.dot_general(image_rows.reshape(dev_count * chunk, pair_total * block_...]
    all_to_all x1 -> x2, waiting for transfers between devices: 27.5 us -> 17.3 us  [on_device(): lax.all_to_all(chi_part.reshape(dev_count, chunk, aux_total), ('row', 'co...]
    all_to_all x2, waiting for transfers between devices: 91.7 us -> 83.8 us  [on_device(): lax.all_to_all(image_blocks, ('row', 'col'), split_axis=2, concat_axis=0,...]
    dot_general x1 -> x2, matrix products: 11.4 us -> 15.7 us  [on_device(): lax.dot_general(image_rows.reshape(dev_count * chunk, pair_total * block_...]
  transfers between devices with their start and end apart: 7 -> 8, of which waited for: 7 -> 8; matrix products, arithmetic and copies ran while one was open for 33% -> 38% of each run, Pallas kernels for 0% -> 0%
where the time goes in v3:
time: 585 us; the launch traced here: 575 us
  waiting for transfers between devices  311 us (53%)
  local copies, waits for them, and re-layouts  167 us (29%)
  matrix products  49.3 us (8%)
  starting transfers between devices  35.6 us (6%)
  other arithmetic  11.3 us (2%)
    all_to_all x2, waiting for transfers between devices, on_device(): lax.all_to_all(grouped[:, :, part].reshape(slots.shape[0], col_count * ch...  163 us
    all_to_all x2, waiting for transfers between devices, on_device(): lax.all_to_all(image_blocks, ('row', 'col'), split_axis=2, concat_axis=0,...  83.8 us
    all_to_all x2, waiting for transfers between devices, on_device(): lax.all_to_all(x_compact, ('row', 'col'), split_axis=2, concat_axis=0, ti...  47.3 us
    reshape x4, local copies, waits for them, and re-layouts, on_device(): image_blocks.reshape(chunk, pair_total, dev_count, block_span)  28.1 us
    reshape x4, local copies, waits for them, and re-layouts, on_device(): contracted.reshape(chunk, NBLK, B, NBLK, B).transpose(0, 1, 3, 2, 4)  24.5 us
    dot_general x2, matrix products, on_device(): jnp.einsum('pln,ns->pls', half_done, masked[1], preferred_element_type=jn...  18 us
    all_to_all x2, waiting for transfers between devices, on_device(): lax.all_to_all(chi_part.reshape(dev_count, chunk, aux_total), ('row', 'co...  17.3 us
    dot_general x2, matrix products, on_device(): lax.dot_general(image_rows.reshape(dev_count * chunk, pair_total * block_...  15.7 us
  transfers between devices with their start and end apart: 8, of which 8 were waited for; matrix products, arithmetic and copies ran while one was open for 38% of the time, Pallas kernels for 0%

profile of v3, /device:TPU:0, one launch (start us, length us, event | category | flops | bytes accessed | tf_op | source)
XLA Modules:
  0.0 575.4 jit_solution(11637416609927592440)
XLA Ops:
  0.0 5.2 fusion.33
  7.5 7.3 %all-to-all-start.3 = ((bf16[2,64,128,128]{3,2,0,1:T(8,128)(2,1)}), bf16[2,64,128,128]{3,2,0,1:T(8,128)(2,1)}, u32[]{:S(2)}, u32[]{:S(2)}) async-start(bf16[2,64,128,128]{3,2,0,1:T(8,128)(2,1)} %bitcast.136), calls=%async_computation.3 | async-start | bytes 8388608 | tf_op jit(solution)/shard_map/all_to_all | solution.py:24
  14.7 4.7 copy.98
  19.5 88.5 %all-to-all-done.3 = bf16[2,64,128,128]{3,2,0,1:T(8,128)(2,1)} async-done(((bf16[2,64,128,128]{3,2,0,1:T(8,128)(2,1)}), bf16[2,64,128,128]{3,2,0,1:T(8,128)(2,1)}, u32[]{:S(2)}, u32[]{:S(2)}) %all-to-all-start.3) | async-done | bytes 4194336 | tf_op jit(solution)/shard_map/all_to_all | solution.py:24
  112.9 6.5 %copy.79 = bf16[8,2,8,128,128]{4,1,0,3,2:T(2,128)(2,1)S(1)} copy(bf16[8,2,8,128,128]{4,3,1,2,0:T(8,128)(2,1)} %bitcast.35) | data formatting | bytes 8388608 | tf_op jit(solution)/shard_map/all_to_all | solution.py:24
  130.7 74.6 %all-to-all-done = bf16[2,64,128,128]{3,2,0,1:T(8,128)(2,1)} async-done(((bf16[2,64,128,128]{3,2,0,1:T(8,128)(2,1)}), bf16[2,64,128,128]{3,2,0,1:T(8,128)(2,1)}, u32[]{:S(2)}, u32[]{:S(2)}) %all-to-all-start) | async-done | bytes 4194336 | tf_op jit(solution)/shard_map/all_to_all | solution.py:24
  209.6 6.5 %copy.68 = bf16[8,2,8,128,128]{4,1,0,3,2:T(2,128)(2,1)S(1)} copy(bf16[8,2,8,128,128]{4,3,1,2,0:T(8,128)(2,1)} %bitcast.7) | data formatting | bytes 8388608 | tf_op jit(solution)/shard_map/all_to_all | solution.py:24
  227.4 43.4 %all-to-all-done.4 = bf16[8,10,32,512]{3,0,1,2:T(8,128)(2,1)} async-done(((bf16[8,10,32,512]{3,0,1,2:T(8,128)(2,1)}), bf16[8,10,32,512]{3,0,1,2:T(8,128)(2,1)}, u32[]{:S(2)}, u32[]{:S(2)}) %all-to-all-start.4) | async-done | bytes 2621472 | tf_op jit(solution)/shard_map/all_to_all | solution.py:63
  289.6 7.3 %reshape.93 = bf16[8,512,512]{2,1,0:T(8,128)(2,1)} reshape(bf16[8,4,128,4,128]{4,3,2,1,0:T(4,128)(2,1)} %bitcast.140) | data formatting | bytes 8388608 | tf_op jit(solution)/shard_map/reshape | solution.py:70
  296.8 9.0 %fusion.6 = bf16[8,512,512]{2,1,0:T(8,128)(2,1)} fusion(bf16[8,512,512]{2,1,0:T(8,128)(2,1)} %reshape.93, bf16[2,512,512]{2,1,0:T(8,128)(2,1)} %mul.32), kind=kOutput, calls=%fused_computation.15 | convolution fusion | flops 4299161600 | bytes 9437184 | tf_op jit(solution)/shard_map/pln,ns->pls/dot_general | solution.py:74
  305.8 7.0 %reshape.94 = bf16[8,4,128,4,128]{4,3,2,1,0:T(4,128)(2,1)} reshape(bf16[8,512,512]{2,1,0:T(8,128)(2,1)} %fusion.6) | data formatting | bytes 8388608 | tf_op jit(solution)/shard_map/reshape | solution.py:77
  312.8 5.3 copy.106
  318.1 7.5 %reshape.95 = bf16[8,16,32,512]{3,2,1,0:T(8,128)(2,1)} reshape(bf16[8,4,4,128,128]{4,3,2,1,0:T(8,128)(2,1)} %bitcast.141) | data formatting | bytes 8388608 | tf_op jit(solution)/shard_map/reshape | solution.py:78
  325.7 6.5 %copy.73 = bf16[8,16,32,512]{3,1,0,2:T(8,128)(2,1)} copy(bf16[8,16,32,512]{3,2,1,0:T(8,128)(2,1)} %reshape.95) | data formatting | bytes 8388608 | tf_op jit(solution)/shard_map/reshape | solution.py:78
  347.6 7.2 %reshape.104 = bf16[8,512,512]{2,1,0:T(8,128)(2,1)} reshape(bf16[8,4,128,4,128]{4,3,2,1,0:T(4,128)(2,1)} %bitcast.142) | data formatting | bytes 8388608 | tf_op jit(solution)/shard_map/reshape | solution.py:70
  354.8 9.0 %fusion.9 = bf16[8,512,512]{2,1,0:T(8,128)(2,1)} fusion(bf16[8,512,512]{2,1,0:T(8,128)(2,1)} %reshape.104, bf16[2,512,512]{2,1,0:T(8,128)(2,1)} %mul.32), kind=kOutput, calls=%fused_computation.16 | convolution fusion | flops 4299161600 | bytes 9437184 | tf_op jit(solution)/shard_map/pln,ns->pls/dot_general | solution.py:74
  363.8 6.9 %reshape.105 = bf16[8,4,128,4,128]{4,3,2,1,0:T(4,128)(2,1)} reshape(bf16[8,512,512]{2,1,0:T(8,128)(2,1)} %fusion.9) | data formatting | bytes 8388608 | tf_op jit(solution)/shard_map/reshape | solution.py:77
  370.7 5.3 copy.104
  376.1 7.5 %reshape.106 = bf16[8,16,32,512]{3,2,1,0:T(8,128)(2,1)} reshape(bf16[8,4,4,128,128]{4,3,2,1,0:T(8,128)(2,1)} %bitcast.143) | data formatting | bytes 8388608 | tf_op jit(solution)/shard_map/reshape | solution.py:78
  383.6 6.5 %copy.88 = bf16[8,16,32,512]{3,1,0,2:T(8,128)(2,1)} copy(bf16[8,16,32,512]{3,2,1,0:T(8,128)(2,1)} %reshape.106) | data formatting | bytes 8388608 | tf_op jit(solution)/shard_map/reshape | solution.py:78
  390.1 45.0 %all-to-all-done.1 = bf16[8,16,32,512]{3,1,0,2:T(8,128)(2,1)} async-done(((bf16[8,16,32,512]{3,1,0,2:T(8,128)(2,1)}), bf16[8,16,32,512]{3,1,0,2:T(8,128)(2,1)}, u32[]{:S(2)}, u32[]{:S(2)}) %all-to-all-start.1) | async-done | bytes 4194336 | tf_op jit(solution)/shard_map/all_to_all | solution.py:79
  445.6 7.4 %reshape.101 = bf16[32,1,8,8192]{3,2,0,1:T(8,128)(2,1)} reshape(bf16[4,64,16,512]{3,2,1,0:T(8,128)(2,1)} %convert_bitcast_fusion) | data formatting | bytes 8388608 | tf_op jit(solution)/shard_map/reshape | solution.py:87
  457.7 7.5 %reshape.98 = bf16[32,1,8,8192]{3,2,0,1:T(8,128)(2,1)} reshape(bf16[4,64,16,512]{3,2,1,0:T(8,128)(2,1)} %convert_bitcast_fusion.2) | data formatting | bytes 8388608 | tf_op jit(solution)/shard_map/reshape | solution.py:87
  465.1 7.5 %pad_maximum_fusion = bf16[32,2,8,8192]{3,2,0,1:T(8,128)(2,1)} fusion(bf16[32,1,8,8192]{3,2,0,1:T(8,128)(2,1)} %reshape.101, bf16[32,1,8,8192]{3,2,0,1:T(8,128)(2,1)} %reshape.98), kind=kLoop, calls=%fused_computation | loop fusion | flops 4194304 | bytes 16777216 | tf_op jit(solution)/shard_map/concatenate | solution.py:90
  472.6 7.6 %copy.83 = bf16[32,2,8,8192]{3,2,1,0:T(8,128)(2,1)} copy(bf16[32,2,8,8192]{3,2,0,1:T(8,128)(2,1)} %pad_maximum_fusion) | data formatting | bytes 16777216 | tf_op jit(solution)/shard_map/concatenate | solution.py:90
  480.2 7.4 %dot_general.43 = bf16[32,8,8192]{2,1,0:T(8,128)(2,1)} reshape(bf16[32,8,16,1,512]{4,2,1,0,3:T(8,128)(2,1)} %bitcast.19) | data formatting | bytes 8388608 | tf_op jit(solution)/shard_map/dot_general | solution.py:93
  487.6 7.8 %fusion.34 = f32[32,8,512]{2,1,0:T(8,128)} fusion(bf16[32,8,8192]{2,1,0:T(8,128)(2,1)} %dot_general.43, bf16[512,8192,1]{1,0,2:T(8,128)(2,1)} %bitcast.147), kind=kOutput, calls=%fused_computation.49 | convolution fusion | flops 2147483648 | bytes 13107200 | tf_op jit(solution)/shard_map/dot_general | solution.py:93
  495.4 38.8 %all-to-all-done.6 = bf16[8,16,32,512]{3,1,0,2:T(8,128)(2,1)} async-done(((bf16[8,16,32,512]{3,1,0,2:T(8,128)(2,1)}), bf16[8,16,32,512]{3,1,0,2:T(8,128)(2,1)}, u32[]{:S(2)}, u32[]{:S(2)}) %all-to-all-start.6) | async-done | bytes 4194336 | tf_op jit(solution)/shard_map/all_to_all | solution.py:79
  537.0 7.4 %dot_general.52 = bf16[32,8,8192]{2,1,0:T(8,128)(2,1)} reshape(bf16[32,8,16,1,512]{4,2,1,0,3:T(8,128)(2,1)} %bitcast.51) | data formatting | bytes 8388608 | tf_op jit(solution)/shard_map/dot_general | solution.py:93
  544.4 7.8 %fusion.35 = f32[32,8,512]{2,1,0:T(8,128)} fusion(bf16[32,8,8192]{2,1,0:T(8,128)(2,1)} %dot_general.52, bf16[512,8192,1]{1,0,2:T(8,128)(2,1)} %bitcast.148), kind=kOutput, calls=%fused_computation.50 | convolution fusion | flops 2147483648 | bytes 13107200 | tf_op jit(solution)/shard_map/dot_general | solution.py:93
  553.3 4.9 all-to-all-start.7
  558.3 16.2 %all-to-all-done.7 = f32[32,8,512]{2,1,0:T(8,128)S(1)} async-done(((f32[32,8,512]{2,1,0:T(8,128)}), f32[32,8,512]{2,1,0:T(8,128)S(1)}, u32[]{:S(2)}, u32[]{:S(2)}) %all-to-all-start.7) | async-done | bytes 524320 | tf_op jit(solution)/shard_map/all_to_all | solution.py:99
  (52 shorter events, 87.9 us)
Async XLA Ops:
  7.5 100.5 %all-to-all-start.3 = ((bf16[2,64,128,128]{3,2,0,1:T(8,128)(2,1)}), bf16[2,64,128,128]{3,2,0,1:T(8,128)(2,1)}, u32[]{:S(2)}, u32[]{:S(2)}) async-start(bf16[2,64,128,128]{3,2,0,1:T(8,128)(2,1)} %bitcast.136), calls=%async_computation.3 | async-start | bytes 8388608 | tf_op jit(solution)/shard_map/all_to_all | solution.py:24
  108.0 4.7 copy-start.2
  108.0 97.2 %all-to-all-start = ((bf16[2,64,128,128]{3,2,0,1:T(8,128)(2,1)}), bf16[2,64,128,128]{3,2,0,1:T(8,128)(2,1)}, u32[]{:S(2)}, u32[]{:S(2)}) async-start(bf16[2,64,128,128]{3,2,0,1:T(8,128)(2,1)} %bitcast.135), calls=%async_computation | async-start | bytes 8388608 | tf_op jit(solution)/shard_map/all_to_all | solution.py:24
  119.4 2.0 copy-start
  205.3 65.6 %all-to-all-start.4 = ((bf16[8,10,32,512]{3,0,1,2:T(8,128)(2,1)}), bf16[8,10,32,512]{3,0,1,2:T(8,128)(2,1)}, u32[]{:S(2)}, u32[]{:S(2)}) async-start(bf16[8,10,32,512]{3,0,1,2:T(8,128)(2,1)} %copy.81), calls=%async_computation.4 | async-start | bytes 5242880 | tf_op jit(solution)/shard_map/all_to_all | solution.py:63
  216.1 2.0 copy-start.1
  224.5 50.2 %copy-start.3 = (s32[2,4,4]{2,1,0:T(4,128)S(1)}, s32[2,4,4]{2,1,0:T(4,128)}, u32[]{:S(2)}) copy-start(s32[2,4,4]{2,1,0:T(4,128)} %param.8) | copy-start | bytes 388
  270.9 65.1 %all-to-all-start.2 = ((bf16[8,10,32,512]{3,0,1,2:T(8,128)(2,1)}), bf16[8,10,32,512]{3,0,1,2:T(8,128)(2,1)S(1)}, u32[]{:S(2)}, u32[]{:S(2)}) async-start(bf16[8,10,32,512]{3,0,1,2:T(8,128)(2,1)} %copy.75), calls=%async_computation.2 | async-start | bytes 5242880 | tf_op jit(solution)/shard_map/all_to_all | solution.py:63
  336.0 99.1 %all-to-all-start.1 = ((bf16[8,16,32,512]{3,1,0,2:T(8,128)(2,1)}), bf16[8,16,32,512]{3,1,0,2:T(8,128)(2,1)}, u32[]{:S(2)}, u32[]{:S(2)}) async-start(bf16[8,16,32,512]{3,1,0,2:T(8,128)(2,1)} %copy.73), calls=%async_computation.1 | async-start | bytes 8388608 | tf_op jit(solution)/shard_map/all_to_all | solution.py:79
  435.1 99.1 %all-to-all-start.6 = ((bf16[8,16,32,512]{3,1,0,2:T(8,128)(2,1)}), bf16[8,16,32,512]{3,1,0,2:T(8,128)(2,1)}, u32[]{:S(2)}, u32[]{:S(2)}) async-start(bf16[8,16,32,512]{3,1,0,2:T(8,128)(2,1)} %copy.88), calls=%async_computation.6 | async-start | bytes 8388608 | tf_op jit(solution)/shard_map/all_to_all | solution.py:79
  534.2 19.1 %all-to-all-start.5 = ((f32[32,8,512]{2,1,0:T(8,128)}), f32[32,8,512]{2,1,0:T(8,128)S(1)}, u32[]{:S(2)}, u32[]{:S(2)}) async-start(f32[32,8,512]{2,1,0:T(8,128)} %fusion.34), calls=%async_computation.5 | async-start | bytes 1048576 | tf_op jit(solution)/shard_map/all_to_all | solution.py:99
  544.4 13.8 %copy-start.4 = (s32[1,4]{1,0:T(1,128)S(1)}, s32[1,4]{1,0:T(1,128)}, u32[]{:S(2)}) copy-start(s32[1,4]{1,0:T(1,128)} %param.9) | copy-start | bytes 52
  553.3 21.2 %all-to-all-start.7 = ((f32[32,8,512]{2,1,0:T(8,128)}), f32[32,8,512]{2,1,0:T(8,128)S(1)}, u32[]{:S(2)}, u32[]{:S(2)}) async-start(f32[32,8,512]{2,1,0:T(8,128)} %fusion.35), calls=%async_computation.7 | async-start | bytes 1048576 | tf_op jit(solution)/shard_map/all_to_all | solution.py:99

commit v4 on v3

--- a/solution.py
+++ b/solution.py
@@ -19,10 +19,10 @@
     row_index = lax.axis_index("row")
     slots = x_slots[0]
     chunk = slots.shape[1] // (col_count * CHUNKS)
-    grouped = slots.reshape(slots.shape[0], col_count, CHUNKS, chunk, B, B)
+    group = col_count * chunk
     arrivals = [
         lax.all_to_all(
-            grouped[:, :, part].reshape(slots.shape[0], col_count * chunk, B, B),
+            slots[:, part * group : (part + 1) * group],
             "col",
             split_axis=1,
             concat_axis=0,
@@ -79,32 +79,39 @@
         image_rows = lax.all_to_all(
             image_blocks, ("row", "col"), split_axis=2, concat_axis=0, tiled=True
         )
-        compact_rows = compact_rows.reshape(row_count, col_count * chunk, NNZ, block_span)
+        compact_rows = compact_rows.reshape(row_count, group, NNZ, block_span)
         dense_rows = jnp.einsum(
             "rjk,rqjz->rqkz", expand, compact_rows, preferred_element_type=jnp.float32
         ).astype(jnp.bfloat16)
-        image_rows = image_rows.reshape(dev_count, 1, chunk, pair_total * block_span)
-        dense_rows = dense_rows.reshape(dev_count, 1, chunk, pair_total * block_span)
+        image_rows = image_rows.reshape(row_count, 1, group, pair_total * block_span)
+        dense_rows = dense_rows.reshape(row_count, 1, group, pair_total * block_span)
         image_parts.append(image_rows)
         dense_parts.append(dense_rows)
     dense_rows = jnp.concatenate(dense_parts, axis=1).reshape(aux_total, pair_total * block_span)
     chi_sums = []
     for image_rows in image_parts:
         chi_part = lax.dot_general(
-            image_rows.reshape(dev_count * chunk, pair_total * block_span),
+            image_rows.reshape(row_count * group, pair_total * block_span),
             dense_rows,
             (((1,), (1,)), ((), ())),
             preferred_element_type=jnp.float32,
         )
-        chi_parts = lax.all_to_all(
-            chi_part.reshape(dev_count, chunk, aux_total),
-            ("row", "col"),
+        row_parts = lax.all_to_all(
+            chi_part.reshape(row_count, group, aux_total),
+            "row",
             split_axis=0,
             concat_axis=0,
             tiled=True,
         )
-        chi_sums.append(jnp.sum(chi_parts, axis=0))
-    chi_rows = jnp.concatenate(chi_sums, axis=0)
+        chi_sums.append(jnp.sum(row_parts, axis=0))
+    chi_parts = lax.all_to_all(
+        jnp.concatenate(chi_sums, axis=0).reshape(col_count, aux_local, aux_total),
+        "col",
+        split_axis=0,
+        concat_axis=0,
+        tiled=True,
+    )
+    chi_rows = jnp.sum(chi_parts, axis=0)
     column_mask = jnp.repeat(chi_mask[0], AB).astype(jnp.float32)
     return chi_rows * column_mask[None, :]
 

time: 585 us -> 598 us (1.022)
  blocking collectives: 0 us -> 100 us
  waiting for transfers between devices: 311 us -> 223 us
    all_to_all x0 -> x1, blocking collectives: none -> 100 us  [on_device(): lax.all_to_all(slots[:, part * group:(part + 1) * group], 'col', split_ax...]
    all_to_all x4, waiting for transfers between devices: 180 us -> 91.9 us  [the longest x1 74.3 us: on_device(): lax.all_to_all(slots[:, part * group:(part + 1) * group], 'col', split_ax...]
  transfers between devices with their start and end apart: 8 -> 8, of which waited for: 8 -> 7; matrix products, arithmetic and copies ran while one was open for 38% -> 36% of each run, Pallas kernels for 0% -> 0%
where the time goes in v4:
time: 598 us; the launch traced here: 587 us
  waiting for transfers between devices  223 us (37%)
  local copies, waits for them, and re-layouts  171 us (29%)
  blocking collectives  100 us (17%)
  matrix products  49.4 us (8%)
  starting transfers between devices  31.2 us (5%)
  other arithmetic  12 us (2%)
    all_to_all x1, blocking collectives, on_device(): lax.all_to_all(slots[:, part * group:(part + 1) * group], 'col', split_ax...  100 us
    all_to_all x2, waiting for transfers between devices, on_device(): lax.all_to_all(image_blocks, ('row', 'col'), split_axis=2, concat_axis=0,...  83.8 us
    all_to_all x1, waiting for transfers between devices, on_device(): lax.all_to_all(slots[:, part * group:(part + 1) * group], 'col', split_ax...  74.3 us
    all_to_all x2, waiting for transfers between devices, on_device(): lax.all_to_all(x_compact, ('row', 'col'), split_axis=2, concat_axis=0, ti...  47.3 us
    reshape x4, local copies, waits for them, and re-layouts, on_device(): image_blocks.reshape(chunk, pair_total, dev_count, block_span)  28.1 us
    reshape x4, local copies, waits for them, and re-layouts, on_device(): contracted.reshape(chunk, NBLK, B, NBLK, B).transpose(0, 1, 3, 2, 4)  24.5 us
    dot_general x2, matrix products, on_device(): jnp.einsum('pln,ns->pls', half_done, masked[1], preferred_element_type=jn...  18 us
    dot_general x2, matrix products, on_device(): lax.dot_general(image_rows.reshape(row_count * group, pair_total * block_...  15.7 us
  transfers between devices with their start and end apart: 8, of which 7 were waited for; matrix products, arithmetic and copies ran while one was open for 36% of the time, Pallas kernels for 0%

profile of v4, /device:TPU:0, one launch (start us, length us, event | category | flops | bytes accessed | tf_op | source)
XLA Modules:
  0.0 587.1 jit_solution(1692445364145438248)
XLA Ops:
  0.0 10.3 %copy.92 = bf16[1,2,128,128,128]{4,3,1,2,0:T(8,128)(2,1)} copy(bf16[1,2,128,128,128]{4,3,2,1,0:T(8,128)(2,1)} %param.5) | data formatting | bytes 16777216 | tf_op args[0]
  10.3 5.3 fusion.33
  15.7 100.3 %all_to_all.111 = bf16[2,64,128,128]{3,2,0,1:T(8,128)(2,1)} all-to-all(bf16[2,64,128,128]{3,2,0,1:T(8,128)(2,1)S(1)} %get-tuple-element.5), channel_id=1, replica_groups=mesh['row'=4,'col'=8] {'col'}, dimensions={1} | all-to-all | bytes 8388608 | tf_op jit(solution)/shard_map/all_to_all | solution.py:24
  116.0 4.7 all-to-all-start.3
  120.9 6.5 %copy.61 = bf16[2,8,8,128,128]{4,0,1,3,2:T(2,128)(2,1)S(1)} copy(bf16[2,8,8,128,128]{4,3,0,2,1:T(8,128)(2,1)} %bitcast.137) | data formatting | bytes 8388608 | tf_op jit(solution)/shard_map/all_to_all | solution.py:24
  138.7 74.3 %all-to-all-done.3 = bf16[2,64,128,128]{3,2,0,1:T(8,128)(2,1)} async-done(((bf16[2,64,128,128]{3,2,0,1:T(8,128)(2,1)}), bf16[2,64,128,128]{3,2,0,1:T(8,128)(2,1)}, u32[]{:S(2)}, u32[]{:S(2)}) %all-to-all-start.3) | async-done | bytes 4194336 | tf_op jit(solution)/shard_map/all_to_all | solution.py:24
  217.3 6.5 %copy.70 = bf16[2,8,8,128,128]{4,0,1,3,2:T(2,128)(2,1)S(1)} copy(bf16[2,8,8,128,128]{4,3,0,2,1:T(8,128)(2,1)} %bitcast.31) | data formatting | bytes 8388608 | tf_op jit(solution)/shard_map/all_to_all | solution.py:24
  235.2 43.5 %all-to-all-done.2 = bf16[8,10,32,512]{3,0,1,2:T(8,128)(2,1)} async-done(((bf16[8,10,32,512]{3,0,1,2:T(8,128)(2,1)}), bf16[8,10,32,512]{3,0,1,2:T(8,128)(2,1)}, u32[]{:S(2)}, u32[]{:S(2)}) %all-to-all-start.2) | async-done | bytes 2621472 | tf_op jit(solution)/shard_map/all_to_all | solution.py:63
  297.3 7.3 %reshape.96 = bf16[8,512,512]{2,1,0:T(8,128)(2,1)} reshape(bf16[8,4,128,4,128]{4,3,2,1,0:T(4,128)(2,1)} %bitcast.141) | data formatting | bytes 8388608 | tf_op jit(solution)/shard_map/reshape | solution.py:70
  304.6 9.0 %fusion.6 = bf16[8,512,512]{2,1,0:T(8,128)(2,1)} fusion(bf16[8,512,512]{2,1,0:T(8,128)(2,1)} %reshape.96, bf16[2,512,512]{2,1,0:T(8,128)(2,1)} %mul.32), kind=kOutput, calls=%fused_computation.16 | convolution fusion | flops 4299161600 | bytes 9437184 | tf_op jit(solution)/shard_map/pln,ns->pls/dot_general | solution.py:74
  313.6 7.0 %reshape.97 = bf16[8,4,128,4,128]{4,3,2,1,0:T(4,128)(2,1)} reshape(bf16[8,512,512]{2,1,0:T(8,128)(2,1)} %fusion.6) | data formatting | bytes 8388608 | tf_op jit(solution)/shard_map/reshape | solution.py:77
  320.6 5.3 copy.95
  325.9 7.6 %reshape.98 = bf16[8,16,32,512]{3,2,1,0:T(8,128)(2,1)} reshape(bf16[8,4,4,128,128]{4,3,2,1,0:T(8,128)(2,1)} %bitcast.142) | data formatting | bytes 8388608 | tf_op jit(solution)/shard_map/reshape | solution.py:78
  333.4 6.5 %copy.66 = bf16[8,16,32,512]{3,1,0,2:T(8,128)(2,1)} copy(bf16[8,16,32,512]{3,2,1,0:T(8,128)(2,1)} %reshape.98) | data formatting | bytes 8388608 | tf_op jit(solution)/shard_map/reshape | solution.py:78
  355.4 7.2 %reshape.107 = bf16[8,512,512]{2,1,0:T(8,128)(2,1)} reshape(bf16[8,4,128,4,128]{4,3,2,1,0:T(4,128)(2,1)} %bitcast.143) | data formatting | bytes 8388608 | tf_op jit(solution)/shard_map/reshape | solution.py:70
  362.6 9.0 %fusion.9 = bf16[8,512,512]{2,1,0:T(8,128)(2,1)} fusion(bf16[8,512,512]{2,1,0:T(8,128)(2,1)} %reshape.107, bf16[2,512,512]{2,1,0:T(8,128)(2,1)} %mul.32), kind=kOutput, calls=%fused_computation.17 | convolution fusion | flops 4299161600 | bytes 9437184 | tf_op jit(solution)/shard_map/pln,ns->pls/dot_general | solution.py:74
  371.6 6.9 %reshape.108 = bf16[8,4,128,4,128]{4,3,2,1,0:T(4,128)(2,1)} reshape(bf16[8,512,512]{2,1,0:T(8,128)(2,1)} %fusion.9) | data formatting | bytes 8388608 | tf_op jit(solution)/shard_map/reshape | solution.py:77
  378.5 5.3 copy.93
  383.8 7.5 %reshape.109 = bf16[8,16,32,512]{3,2,1,0:T(8,128)(2,1)} reshape(bf16[8,4,4,128,128]{4,3,2,1,0:T(8,128)(2,1)} %bitcast.144) | data formatting | bytes 8388608 | tf_op jit(solution)/shard_map/reshape | solution.py:78
  391.3 6.5 %copy.79 = bf16[8,16,32,512]{3,1,0,2:T(8,128)(2,1)} copy(bf16[8,16,32,512]{3,2,1,0:T(8,128)(2,1)} %reshape.109) | data formatting | bytes 8388608 | tf_op jit(solution)/shard_map/reshape | solution.py:78
  397.8 45.0 %all-to-all-done.1 = bf16[8,16,32,512]{3,1,0,2:T(8,128)(2,1)} async-done(((bf16[8,16,32,512]{3,1,0,2:T(8,128)(2,1)}), bf16[8,16,32,512]{3,1,0,2:T(8,128)(2,1)}, u32[]{:S(2)}, u32[]{:S(2)}) %all-to-all-start.1) | async-done | bytes 4194336 | tf_op jit(solution)/shard_map/all_to_all | solution.py:79
  453.4 7.4 %reshape.101 = bf16[4,1,64,8192]{3,2,0,1:T(8,128)(2,1)} reshape(bf16[4,64,16,512]{3,2,1,0:T(8,128)(2,1)} %convert_bitcast_fusion.2) | data formatting | bytes 8388608 | tf_op jit(solution)/shard_map/reshape | solution.py:87
  465.4 7.5 %reshape.104 = bf16[4,1,64,8192]{3,2,0,1:T(8,128)(2,1)} reshape(bf16[4,64,16,512]{3,2,1,0:T(8,128)(2,1)} %convert_bitcast_fusion) | data formatting | bytes 8388608 | tf_op jit(solution)/shard_map/reshape | solution.py:87
  472.9 7.5 %pad_maximum_fusion = bf16[4,2,64,8192]{3,2,0,1:T(8,128)(2,1)} fusion(bf16[4,1,64,8192]{3,2,0,1:T(8,128)(2,1)} %reshape.104, bf16[4,1,64,8192]{3,2,0,1:T(8,128)(2,1)} %reshape.101), kind=kLoop, calls=%fused_computation | loop fusion | flops 4194304 | bytes 16777216 | tf_op jit(solution)/shard_map/concatenate | solution.py:90
  480.4 7.6 %copy.74 = bf16[4,2,64,8192]{3,2,1,0:T(8,128)(2,1)} copy(bf16[4,2,64,8192]{3,2,0,1:T(8,128)(2,1)} %pad_maximum_fusion) | data formatting | bytes 16777216 | tf_op jit(solution)/shard_map/concatenate | solution.py:90
  488.0 7.4 %dot_general.43 = bf16[4,64,8192]{2,1,0:T(8,128)(2,1)} reshape(bf16[32,8,16,1,512]{4,2,1,0,3:T(8,128)(2,1)} %bitcast.17) | data formatting | bytes 8388608 | tf_op jit(solution)/shard_map/dot_general | solution.py:93
  495.4 7.8 %fusion.34 = f32[4,64,512]{2,1,0:T(8,128)} fusion(bf16[4,64,8192]{2,1,0:T(8,128)(2,1)} %dot_general.43, bf16[512,8192,1]{1,0,2:T(8,128)(2,1)} %bitcast.147), kind=kOutput, calls=%fused_computation.51 | convolution fusion | flops 2147483648 | bytes 13107200 | tf_op jit(solution)/shard_map/dot_general | solution.py:93
  503.2 38.8 %all-to-all-done.6 = bf16[8,16,32,512]{3,1,0,2:T(8,128)(2,1)} async-done(((bf16[8,16,32,512]{3,1,0,2:T(8,128)(2,1)}), bf16[8,16,32,512]{3,1,0,2:T(8,128)(2,1)}, u32[]{:S(2)}, u32[]{:S(2)}) %all-to-all-start.6) | async-done | bytes 4194336 | tf_op jit(solution)/shard_map/all_to_all | solution.py:79
  545.6 7.4 %dot_general.52 = bf16[4,64,8192]{2,1,0:T(8,128)(2,1)} reshape(bf16[32,8,16,1,512]{4,2,1,0,3:T(8,128)(2,1)} %bitcast.49) | data formatting | bytes 8388608 | tf_op jit(solution)/shard_map/dot_general | solution.py:93
  553.0 7.9 %fusion.35 = f32[4,64,512]{2,1,0:T(8,128)} fusion(bf16[4,64,8192]{2,1,0:T(8,128)(2,1)} %dot_general.52, bf16[512,8192,1]{1,0,2:T(8,128)(2,1)} %bitcast.148), kind=kOutput, calls=%fused_computation.52 | convolution fusion | flops 2147483648 | bytes 13107200 | tf_op jit(solution)/shard_map/dot_general | solution.py:93
  564.4 8.8 %all-to-all-done.7 = f32[4,64,512]{2,1,0:T(8,128)S(1)} async-done(((f32[4,64,512]{2,1,0:T(8,128)}), f32[4,64,512]{2,1,0:T(8,128)S(1)}, u32[]{:S(2)}, u32[]{:S(2)}) %all-to-all-start.7) | async-done | bytes 524320 | tf_op jit(solution)/shard_map/all_to_all | solution.py:99
  577.4 8.8 %all-to-all-done.8 = f32[8,16,512]{2,1,0:T(8,128)S(1)} async-done(((f32[8,16,512]{2,1,0:T(8,128)}), f32[8,16,512]{2,1,0:T(8,128)S(1)}, u32[]{:S(2)}, u32[]{:S(2)}) %all-to-all-start.8) | async-done | bytes 262176 | tf_op jit(solution)/shard_map/all_to_all | solution.py:107
  (54 shorter events, 88.4 us)
Async XLA Ops:
  116.0 4.7 copy-start.2
  116.0 97.0 %all-to-all-start.3 = ((bf16[2,64,128,128]{3,2,0,1:T(8,128)(2,1)}), bf16[2,64,128,128]{3,2,0,1:T(8,128)(2,1)}, u32[]{:S(2)}, u32[]{:S(2)}) async-start(bf16[2,64,128,128]{3,2,0,1:T(8,128)(2,1)} %get-tuple-element.6), calls=%async_computation.3 | async-start | bytes 8388608 | tf_op jit(solution)/shard_map/all_to_all | solution.py:24
  127.4 2.0 copy-start.1
  213.0 65.6 %all-to-all-start.2 = ((bf16[8,10,32,512]{3,0,1,2:T(8,128)(2,1)}), bf16[8,10,32,512]{3,0,1,2:T(8,128)(2,1)}, u32[]{:S(2)}, u32[]{:S(2)}) async-start(bf16[8,10,32,512]{3,0,1,2:T(8,128)(2,1)} %copy.68), calls=%async_computation.2 | async-start | bytes 5242880 | tf_op jit(solution)/shard_map/all_to_all | solution.py:63
  223.9 1.9 copy-start
  232.2 50.2 %copy-start.3 = (s32[2,4,4]{2,1,0:T(4,128)S(1)}, s32[2,4,4]{2,1,0:T(4,128)}, u32[]{:S(2)}) copy-start(s32[2,4,4]{2,1,0:T(4,128)} %param.8) | copy-start | bytes 388
  278.7 65.1 %all-to-all-start.4 = ((bf16[8,10,32,512]{3,0,1,2:T(8,128)(2,1)}), bf16[8,10,32,512]{3,0,1,2:T(8,128)(2,1)S(1)}, u32[]{:S(2)}, u32[]{:S(2)}) async-start(bf16[8,10,32,512]{3,0,1,2:T(8,128)(2,1)} %copy.72), calls=%async_computation.4 | async-start | bytes 5242880 | tf_op jit(solution)/shard_map/all_to_all | solution.py:63
  343.8 99.1 %all-to-all-start.1 = ((bf16[8,16,32,512]{3,1,0,2:T(8,128)(2,1)}), bf16[8,16,32,512]{3,1,0,2:T(8,128)(2,1)}, u32[]{:S(2)}, u32[]{:S(2)}) async-start(bf16[8,16,32,512]{3,1,0,2:T(8,128)(2,1)} %copy.66), calls=%async_computation.1 | async-start | bytes 8388608 | tf_op jit(solution)/shard_map/all_to_all | solution.py:79
  442.8 99.1 %all-to-all-start.6 = ((bf16[8,16,32,512]{3,1,0,2:T(8,128)(2,1)}), bf16[8,16,32,512]{3,1,0,2:T(8,128)(2,1)}, u32[]{:S(2)}, u32[]{:S(2)}) async-start(bf16[8,16,32,512]{3,1,0,2:T(8,128)(2,1)} %copy.79), calls=%async_computation.6 | async-start | bytes 8388608 | tf_op jit(solution)/shard_map/all_to_all | solution.py:79
  542.0 18.9 %all-to-all-start.5 = ((f32[4,64,512]{2,1,0:T(8,128)}), f32[4,64,512]{2,1,0:T(8,128)S(1)}, u32[]{:S(2)}, u32[]{:S(2)}) async-start(f32[4,64,512]{2,1,0:T(8,128)} %fusion.34), calls=%async_computation.5 | async-start | bytes 1048576 | tf_op jit(solution)/shard_map/all_to_all | solution.py:99
  553.0 24.3 %copy-start.4 = (s32[1,4]{1,0:T(1,128)S(1)}, s32[1,4]{1,0:T(1,128)}, u32[]{:S(2)}) copy-start(s32[1,4]{1,0:T(1,128)} %param.9) | copy-start | bytes 52
  560.9 12.3 %all-to-all-start.7 = ((f32[4,64,512]{2,1,0:T(8,128)}), f32[4,64,512]{2,1,0:T(8,128)S(1)}, u32[]{:S(2)}, u32[]{:S(2)}) async-start(f32[4,64,512]{2,1,0:T(8,128)} %fusion.35), calls=%async_computation.7 | async-start | bytes 1048576 | tf_op jit(solution)/shard_map/all_to_all | solution.py:99
  573.9 12.4 %all-to-all-start.8 = ((f32[8,16,512]{2,1,0:T(8,128)}), f32[8,16,512]{2,1,0:T(8,128)S(1)}, u32[]{:S(2)}, u32[]{:S(2)}) async-start(f32[8,16,512]{2,1,0:T(8,128)} %bitcast.51), calls=%async_computation.8 | async-start | bytes 524288 | tf_op jit(solution)/shard_map/all_to_all | solution.py:107

commit v5 on v3

--- a/solution.py
+++ b/solution.py
@@ -76,25 +76,28 @@
         ).astype(jnp.bfloat16)
         image_blocks = contracted.reshape(chunk, NBLK, B, NBLK, B).transpose(0, 1, 3, 2, 4)
         image_blocks = image_blocks.reshape(chunk, pair_total, dev_count, block_span)
+        image_blocks = image_blocks.transpose(2, 1, 0, 3)
         image_rows = lax.all_to_all(
-            image_blocks, ("row", "col"), split_axis=2, concat_axis=0, tiled=True
+            image_blocks, ("row", "col"), split_axis=0, concat_axis=0, tiled=True
         )
         compact_rows = compact_rows.reshape(row_count, col_count * chunk, NNZ, block_span)
         dense_rows = jnp.einsum(
             "rjk,rqjz->rqkz", expand, compact_rows, preferred_element_type=jnp.float32
         ).astype(jnp.bfloat16)
-        image_rows = image_rows.reshape(dev_count, 1, chunk, pair_total * block_span)
         dense_rows = dense_rows.reshape(dev_count, 1, chunk, pair_total * block_span)
         image_parts.append(image_rows)
         dense_parts.append(dense_rows)
     dense_rows = jnp.concatenate(dense_parts, axis=1).reshape(aux_total, pair_total * block_span)
     chi_sums = []
     for image_rows in image_parts:
-        chi_part = lax.dot_general(
-            image_rows.reshape(dev_count * chunk, pair_total * block_span),
-            dense_rows,
-            (((1,), (1,)), ((), ())),
-            preferred_element_type=jnp.float32,
+        chi_part = sum(
+            jnp.einsum(
+                "diz,qz->diq",
+                image_rows[:, pair],
+                dense_rows[:, pair * block_span : (pair + 1) * block_span],
+                preferred_element_type=jnp.float32,
+            )
+            for pair in range(pair_total)
         )
         chi_parts = lax.all_to_all(
             chi_part.reshape(dev_count, chunk, aux_total),

time: 585 us -> 595 us (1.017)
  matrix products: 49.3 us -> 80.8 us
  local copies, waits for them, and re-layouts: 167 us -> 152 us
  waiting for transfers between devices: 311 us -> 303 us
    dot_general x2 -> x32, matrix products: 15.7 us -> 47.1 us  [on_device(): jnp.einsum('diz,qz->diq', image_rows[:, pair], dense_rows[:, pair * block...]
    dot_general x2 -> x0, local copies, waits for them, and re-layouts: 14.8 us -> none  [on_device(): lax.dot_general(image_rows.reshape(dev_count * chunk, pair_total * block_...]
    transpose x0 -> x2, local copies, waits for them, and re-layouts: none -> 13 us  [on_device(): image_blocks = image_blocks.transpose(2, 1, 0, 3)]
    reshape x4 -> x2, local copies, waits for them, and re-layouts: 28.1 us -> 15.1 us  [on_device(): image_blocks.reshape(chunk, pair_total, dev_count, block_span)]
    all_to_all x2, waiting for transfers between devices: 83.8 us -> 76.1 us  [on_device(): lax.all_to_all(image_blocks, ('row', 'col'), split_axis=0, concat_axis=0,...]
  transfers between devices with their start and end apart: 8 -> 8, of which waited for: 8 -> 7; matrix products, arithmetic and copies ran while one was open for 38% -> 40% of each run, Pallas kernels for 0% -> 0%
where the time goes in v5:
time: 595 us; the launch traced here: 585 us
  waiting for transfers between devices  303 us (51%)
  local copies, waits for them, and re-layouts  152 us (26%)
  matrix products  80.8 us (14%)
  starting transfers between devices  36.4 us (6%)
  other arithmetic  11.3 us (2%)
    all_to_all x2, waiting for transfers between devices, on_device(): lax.all_to_all(grouped[:, :, part].reshape(slots.shape[0], col_count * ch...  163 us
    all_to_all x2, waiting for transfers between devices, on_device(): lax.all_to_all(image_blocks, ('row', 'col'), split_axis=0, concat_axis=0,...  76.1 us
    all_to_all x2, waiting for transfers between devices, on_device(): lax.all_to_all(x_compact, ('row', 'col'), split_axis=2, concat_axis=0, ti...  47.3 us
    dot_general x32, matrix products, on_device(): jnp.einsum('diz,qz->diq', image_rows[:, pair], dense_rows[:, pair * block...  47.1 us
    reshape x4, local copies, waits for them, and re-layouts, on_device(): contracted.reshape(chunk, NBLK, B, NBLK, B).transpose(0, 1, 3, 2, 4)  24.5 us
    dot_general x2, matrix products, on_device(): jnp.einsum('pln,ns->pls', half_done, masked[1], preferred_element_type=jn...  18 us
    all_to_all x2, waiting for transfers between devices, on_device(): lax.all_to_all(chi_part.reshape(dev_count, chunk, aux_total), ('row', 'co...  16.2 us
    reshape x2, local copies, waits for them, and re-layouts, on_device(): image_blocks.reshape(chunk, pair_total, dev_count, block_span)  15.1 us
  transfers between devices with their start and end apart: 8, of which 7 were waited for; matrix products, arithmetic and copies ran while one was open for 40% of the time, Pallas kernels for 0%

profile of v5, /device:TPU:0, one launch (start us, length us, event | category | flops | bytes accessed | tf_op | source)
XLA Modules:
  0.0 584.6 jit_solution(10518025382004862300)
XLA Ops:
  0.0 5.2 fusion.35
  7.5 7.3 %all-to-all-start = ((bf16[2,64,128,128]{3,2,0,1:T(8,128)(2,1)}), bf16[2,64,128,128]{3,2,0,1:T(8,128)(2,1)}, u32[]{:S(2)}, u32[]{:S(2)}) async-start(bf16[2,64,128,128]{3,2,0,1:T(8,128)(2,1)} %bitcast.374), calls=%async_computation | async-start | bytes 8388608 | tf_op jit(solution)/shard_map/all_to_all | solution.py:24
  14.7 4.7 copy.196
  19.4 88.6 %all-to-all-done = bf16[2,64,128,128]{3,2,0,1:T(8,128)(2,1)} async-done(((bf16[2,64,128,128]{3,2,0,1:T(8,128)(2,1)}), bf16[2,64,128,128]{3,2,0,1:T(8,128)(2,1)}, u32[]{:S(2)}, u32[]{:S(2)}) %all-to-all-start) | async-done | bytes 4194336 | tf_op jit(solution)/shard_map/all_to_all | solution.py:24
  108.0 4.7 all-to-all-start.3
  112.9 6.5 %copy.132 = bf16[8,2,8,128,128]{4,1,0,3,2:T(2,128)(2,1)S(1)} copy(bf16[8,2,8,128,128]{4,3,1,2,0:T(8,128)(2,1)} %bitcast.7) | data formatting | bytes 8388608 | tf_op jit(solution)/shard_map/all_to_all | solution.py:24
  123.6 4.1 reshape.88
  130.7 74.6 %all-to-all-done.3 = bf16[2,64,128,128]{3,2,0,1:T(8,128)(2,1)} async-done(((bf16[2,64,128,128]{3,2,0,1:T(8,128)(2,1)}), bf16[2,64,128,128]{3,2,0,1:T(8,128)(2,1)}, u32[]{:S(2)}, u32[]{:S(2)}) %all-to-all-start.3) | async-done | bytes 4194336 | tf_op jit(solution)/shard_map/all_to_all | solution.py:24
  209.2 6.5 %copy.144 = bf16[8,2,8,128,128]{4,1,0,3,2:T(2,128)(2,1)S(1)} copy(bf16[8,2,8,128,128]{4,3,1,2,0:T(8,128)(2,1)} %bitcast.35) | data formatting | bytes 8388608 | tf_op jit(solution)/shard_map/all_to_all | solution.py:24
  227.1 43.5 %all-to-all-done.2 = bf16[8,10,32,512]{3,0,1,2:T(8,128)(2,1)} async-done(((bf16[8,10,32,512]{3,0,1,2:T(8,128)(2,1)}), bf16[8,10,32,512]{3,0,1,2:T(8,128)(2,1)}, u32[]{:S(2)}, u32[]{:S(2)}) %all-to-all-start.2) | async-done | bytes 2621472 | tf_op jit(solution)/shard_map/all_to_all | solution.py:63
  285.2 4.3 copy.235
  289.5 7.3 %reshape.85 = bf16[8,512,512]{2,1,0:T(8,128)(2,1)} reshape(bf16[8,4,128,4,128]{4,3,2,1,0:T(4,128)(2,1)} %bitcast.378) | data formatting | bytes 8388608 | tf_op jit(solution)/shard_map/reshape | solution.py:70
  296.7 9.0 %fusion.6 = bf16[8,512,512]{2,1,0:T(8,128)(2,1)} fusion(bf16[8,512,512]{2,1,0:T(8,128)(2,1)} %reshape.85, bf16[2,512,512]{2,1,0:T(8,128)(2,1)} %mul.32), kind=kOutput, calls=%fused_computation.15 | convolution fusion | flops 4299161600 | bytes 9437184 | tf_op jit(solution)/shard_map/pln,ns->pls/dot_general | solution.py:74
  305.7 7.0 %reshape.86 = bf16[8,4,128,4,128]{4,3,2,1,0:T(4,128)(2,1)} reshape(bf16[8,512,512]{2,1,0:T(8,128)(2,1)} %fusion.6) | data formatting | bytes 8388608 | tf_op jit(solution)/shard_map/reshape | solution.py:77
  312.7 5.3 copy.234
  318.0 7.6 %reshape.87 = bf16[8,16,32,512]{3,2,1,0:T(8,128)(2,1)} reshape(bf16[8,4,4,128,128]{4,3,2,1,0:T(8,128)(2,1)} %bitcast.379) | data formatting | bytes 8388608 | tf_op jit(solution)/shard_map/reshape | solution.py:78
  325.6 6.5 %copy.137 = bf16[32,16,8,512]{3,2,1,0:T(8,128)(2,1)} copy(bf16[32,16,8,512]{3,0,1,2:T(8,128)(2,1)} %bitcast.380) | data formatting | bytes 8388608 | tf_op jit(solution)/shard_map/transpose | solution.py:79
  343.2 4.3 copy.233
  347.5 7.2 %reshape.96 = bf16[8,512,512]{2,1,0:T(8,128)(2,1)} reshape(bf16[8,4,128,4,128]{4,3,2,1,0:T(4,128)(2,1)} %bitcast.381) | data formatting | bytes 8388608 | tf_op jit(solution)/shard_map/reshape | solution.py:70
  354.7 9.0 %fusion.9 = bf16[8,512,512]{2,1,0:T(8,128)(2,1)} fusion(bf16[8,512,512]{2,1,0:T(8,128)(2,1)} %reshape.96, bf16[2,512,512]{2,1,0:T(8,128)(2,1)} %mul.32), kind=kOutput, calls=%fused_computation.16 | convolution fusion | flops 4299161600 | bytes 9437184 | tf_op jit(solution)/shard_map/pln,ns->pls/dot_general | solution.py:74
  363.7 6.9 %reshape.97 = bf16[8,4,128,4,128]{4,3,2,1,0:T(4,128)(2,1)} reshape(bf16[8,512,512]{2,1,0:T(8,128)(2,1)} %fusion.9) | data formatting | bytes 8388608 | tf_op jit(solution)/shard_map/reshape | solution.py:77
  370.6 5.3 copy.232
  375.9 7.5 %reshape.98 = bf16[8,16,32,512]{3,2,1,0:T(8,128)(2,1)} reshape(bf16[8,4,4,128,128]{4,3,2,1,0:T(8,128)(2,1)} %bitcast.382) | data formatting | bytes 8388608 | tf_op jit(solution)/shard_map/reshape | solution.py:78
  383.4 6.5 %copy.168 = bf16[32,16,8,512]{3,2,1,0:T(8,128)(2,1)} copy(bf16[32,16,8,512]{3,0,1,2:T(8,128)(2,1)} %bitcast.383) | data formatting | bytes 8388608 | tf_op jit(solution)/shard_map/transpose | solution.py:79
  389.9 45.0 %all-to-all-done.1 = bf16[32,16,8,512]{3,2,1,0:T(8,128)(2,1)} async-done(((bf16[32,16,8,512]{3,2,1,0:T(8,128)(2,1)}), bf16[32,16,8,512]{3,2,1,0:T(8,128)(2,1)}, u32[]{:S(2)}, u32[]{:S(2)}) %all-to-all-start.1) | async-done | bytes 4194336 | tf_op jit(solution)/shard_map/all_to_all | solution.py:80
  445.3 7.4 %reshape.90 = bf16[32,1,8,8192]{3,2,0,1:T(8,128)(2,1)} reshape(bf16[4,64,16,512]{3,2,1,0:T(8,128)(2,1)} %convert_bitcast_fusion.2) | data formatting | bytes 8388608 | tf_op jit(solution)/shard_map/reshape | solution.py:87
  457.3 7.5 %reshape.93 = bf16[32,1,8,8192]{3,2,0,1:T(8,128)(2,1)} reshape(bf16[4,64,16,512]{3,2,1,0:T(8,128)(2,1)} %convert_bitcast_fusion) | data formatting | bytes 8388608 | tf_op jit(solution)/shard_map/reshape | solution.py:87
  464.8 7.5 %pad_maximum_fusion = bf16[32,2,8,8192]{3,2,0,1:T(8,128)(2,1)} fusion(bf16[32,1,8,8192]{3,2,0,1:T(8,128)(2,1)} %reshape.93, bf16[32,1,8,8192]{3,2,0,1:T(8,128)(2,1)} %reshape.90), kind=kLoop, calls=%fused_computation | loop fusion | flops 4194304 | bytes 16777216 | tf_op jit(solution)/shard_map/concatenate | solution.py:90
  472.3 7.6 %copy.148 = bf16[32,2,8,8192]{3,2,1,0:T(8,128)(2,1)} copy(bf16[32,2,8,8192]{3,2,0,1:T(8,128)(2,1)} %pad_maximum_fusion) | data formatting | bytes 16777216 | tf_op jit(solution)/shard_map/concatenate | solution.py:90
  502.8 31.1 %all-to-all-done.6 = bf16[32,16,8,512]{3,2,1,0:T(8,128)(2,1)} async-done(((bf16[32,16,8,512]{3,2,1,0:T(8,128)(2,1)}), bf16[32,16,8,512]{3,2,1,0:T(8,128)(2,1)}, u32[]{:S(2)}, u32[]{:S(2)}) %all-to-all-start.6) | async-done | bytes 4194336 | tf_op jit(solution)/shard_map/all_to_all | solution.py:80
  561.1 5.9 %all-to-all-start.7 = ((f32[32,8,512]{2,1,0:T(8,128)}), f32[32,8,512]{2,1,0:T(8,128)S(1)}, u32[]{:S(2)}, u32[]{:S(2)}) async-start(f32[32,8,512]{2,1,0:T(8,128)} %convolution_add_fusion), calls=%async_computation.7 | async-start | bytes 1048576 | tf_op jit(solution)/shard_map/all_to_all | solution.py:102
  567.2 16.2 %all-to-all-done.7 = f32[32,8,512]{2,1,0:T(8,128)S(1)} async-done(((f32[32,8,512]{2,1,0:T(8,128)}), f32[32,8,512]{2,1,0:T(8,128)S(1)}, u32[]{:S(2)}, u32[]{:S(2)}) %all-to-all-start.7) | async-done | bytes 524320 | tf_op jit(solution)/shard_map/all_to_all | solution.py:102
  (82 shorter events, 116.3 us)
Async XLA Ops:
  7.5 100.5 %all-to-all-start = ((bf16[2,64,128,128]{3,2,0,1:T(8,128)(2,1)}), bf16[2,64,128,128]{3,2,0,1:T(8,128)(2,1)}, u32[]{:S(2)}, u32[]{:S(2)}) async-start(bf16[2,64,128,128]{3,2,0,1:T(8,128)(2,1)} %bitcast.374), calls=%async_computation | async-start | bytes 8388608 | tf_op jit(solution)/shard_map/all_to_all | solution.py:24
  108.0 4.7 copy-start.3
  108.0 97.2 %all-to-all-start.3 = ((bf16[2,64,128,128]{3,2,0,1:T(8,128)(2,1)}), bf16[2,64,128,128]{3,2,0,1:T(8,128)(2,1)}, u32[]{:S(2)}, u32[]{:S(2)}) async-start(bf16[2,64,128,128]{3,2,0,1:T(8,128)(2,1)} %bitcast.373), calls=%async_computation.3 | async-start | bytes 8388608 | tf_op jit(solution)/shard_map/all_to_all | solution.py:24
  119.4 2.0 copy-start.2
  205.2 65.3 %all-to-all-start.2 = ((bf16[8,10,32,512]{3,0,1,2:T(8,128)(2,1)}), bf16[8,10,32,512]{3,0,1,2:T(8,128)(2,1)}, u32[]{:S(2)}, u32[]{:S(2)}) async-start(bf16[8,10,32,512]{3,0,1,2:T(8,128)(2,1)} %copy.140), calls=%async_computation.2 | async-start | bytes 5242880 | tf_op jit(solution)/shard_map/all_to_all | solution.py:63
  215.8 2.0 copy-start.1
  224.1 50.5 %copy-start.4 = (s32[2,4,4]{2,1,0:T(4,128)S(1)}, s32[2,4,4]{2,1,0:T(4,128)}, u32[]{:S(2)}) copy-start(s32[2,4,4]{2,1,0:T(4,128)} %param.8) | copy-start | bytes 388
  270.6 65.3 %all-to-all-start.4 = ((bf16[8,10,32,512]{3,0,1,2:T(8,128)(2,1)}), bf16[8,10,32,512]{3,0,1,2:T(8,128)(2,1)S(1)}, u32[]{:S(2)}, u32[]{:S(2)}) async-start(bf16[8,10,32,512]{3,0,1,2:T(8,128)(2,1)} %copy.146), calls=%async_computation.4 | async-start | bytes 5242880 | tf_op jit(solution)/shard_map/all_to_all | solution.py:63
  335.9 99.0 %all-to-all-start.1 = ((bf16[32,16,8,512]{3,2,1,0:T(8,128)(2,1)}), bf16[32,16,8,512]{3,2,1,0:T(8,128)(2,1)}, u32[]{:S(2)}, u32[]{:S(2)}) async-start(bf16[32,16,8,512]{3,2,1,0:T(8,128)(2,1)} %copy.137), calls=%async_computation.1 | async-start | bytes 8388608 | tf_op jit(solution)/shard_map/all_to_all | solution.py:80
  434.9 98.9 %all-to-all-start.6 = ((bf16[32,16,8,512]{3,2,1,0:T(8,128)(2,1)}), bf16[32,16,8,512]{3,2,1,0:T(8,128)(2,1)}, u32[]{:S(2)}, u32[]{:S(2)}) async-start(bf16[32,16,8,512]{3,2,1,0:T(8,128)(2,1)} %copy.168), calls=%async_computation.6 | async-start | bytes 8388608 | tf_op jit(solution)/shard_map/all_to_all | solution.py:80
  479.8 7.9 %copy-start = (bf16[32,2,8,8192]{3,2,1,0:T(8,128)(2,1)S(1)}, bf16[32,2,8,8192]{3,2,1,0:T(8,128)(2,1)}, u32[]{:S(2)}) copy-start(bf16[32,2,8,8192]{3,2,1,0:T(8,128)(2,1)} %copy.148) | copy-start | bytes 25165828
  533.9 27.3 %all-to-all-start.5 = ((f32[32,8,512]{2,1,0:T(8,128)}), f32[32,8,512]{2,1,0:T(8,128)S(1)}, u32[]{:S(2)}, u32[]{:S(2)}) async-start(f32[32,8,512]{2,1,0:T(8,128)} %convolution_add_fusion.15), calls=%async_computation.5 | async-start | bytes 1048576 | tf_op jit(solution)/shard_map/all_to_all | solution.py:102
  554.4 12.7 %copy-start.5 = (s32[1,4]{1,0:T(1,128)S(1)}, s32[1,4]{1,0:T(1,128)}, u32[]{:S(2)}) copy-start(s32[1,4]{1,0:T(1,128)} %param.9) | copy-start | bytes 52
  561.1 22.3 %all-to-all-start.7 = ((f32[32,8,512]{2,1,0:T(8,128)}), f32[32,8,512]{2,1,0:T(8,128)S(1)}, u32[]{:S(2)}, u32[]{:S(2)}) async-start(f32[32,8,512]{2,1,0:T(8,128)} %convolution_add_fusion), calls=%async_computation.7 | async-start | bytes 1048576 | tf_op jit(solution)/shard_map/all_to_all | solution.py:102
